TPU v7x, 256 devices: a whole 4x4x8 slice. The times are simulated.
256 devices in a mesh: expert: 64 (over z, x, core), mp: 4 (over y).
Axes of the slice: x: 4, y: 4, z: 8, core: 2. Of those that a mesh axis runs over, the one named last changes fastest.
Arguments:
- tokens: bfloat16 [64, 1024, 6144], P('expert', None, 'mp'), may hold values from -6 to 6
- cotangent: bfloat16 [64, 1024, 256], P('expert')
- counts: int32 [64], P('expert'), may hold values from 1 to 1024, as said below
- place_now: int32 [64], replicated, may hold values from 0 to 31, as said below
- partner: int32 [64], replicated, may hold values from 0 to 63, as said below
- place_next: int32 [64], replicated, may hold values from 0 to 31, as said below
- weight: float32 [64, 6144, 256], P('expert', 'mp'), as said below
- first_moment: float32 [64, 6144, 256], P('expert', 'mp'), as said below
- second_moment: float32 [64, 6144, 256], P('expert', 'mp'), as said below
Outputs:
- new_weight: float32 [64, 6144, 256], P('expert', 'mp')
- new_first: float32 [64, 6144, 256], P('expert', 'mp')
- new_second: float32 [64, 6144, 256], P('expert', 'mp')
Inputs may be any that keep to these rules, and one draw needn't show every extreme that they name: `counts`: some slot has exactly 1024 live rows in every draw. `place_now`: every one of the 32 shards is held by exactly two slots. partner[s] is the other slot holding place_now[s]; partner[partner[s]] = s. `place_next`: every one of the 32 shards is held by exactly two slots. `weight`: slots holding the same shard in place_now have equal weights and moments. `first_moment`: slots holding the same shard in place_now have equal weights and moments. `second_moment`: Positive; slots holding the same shard in place_now have equal values.
All inputs are finite; a program needn't handle non-finite values.
Results may differ from a plain program's by a relative error of at most 0.0003.
Values sent between devices are 32-bit elements; how exact they have to be, the bound alone decides.
No kernel may reach another device: no remote copies, remote signals or barrier semaphores. Data moves between devices by JAX's collectives and lax.ppermute only.
A program may use at most 64 MiB of HBM per device.

v0:
```python
import math

import jax
import jax.numpy as jnp
from jax import lax
from jax.sharding import PartitionSpec as P


def local_grad(block, grad_rows, live):
    rows_total = block.shape[0]
    row_ids = jnp.arange(rows_total, dtype=jnp.int32)
    masked = jnp.where((row_ids < live)[:, None], grad_rows, jnp.zeros_like(grad_rows))
    return jnp.einsum("rd,rh->dh", block, masked, preferred_element_type=jnp.float32)


def clip_scale(partial_sum, limit):
    sumsq = lax.psum(partial_sum, ("expert", "mp"))
    return jnp.minimum(jnp.float32(1.0), limit / jnp.sqrt(sumsq + 1e-06))


def adam_update(total, weights, first, second):
    first_new = 0.9 * first + 0.1 * total
    second_new = 0.95 * second + 0.05 * total * total
    step_size = first_new / (1.0 - 0.9**10) / (jnp.sqrt(second_new / (1.0 - 0.95**10)) + 1e-08)
    return (weights - 0.1 * (step_size + 0.3 * weights), first_new, second_new)


def relay_back(states):
    return (
        lax.all_to_all(states[0], "expert", split_axis=0, concat_axis=0, tiled=True),
        lax.all_to_all(states[1], "expert", split_axis=0, concat_axis=0, tiled=True),
        lax.all_to_all(states[2], "expert", split_axis=0, concat_axis=0, tiled=True),
    )


def on_device(
    tokens, cotangent, counts, place_now, partner, place_next, weight, first_moment, second_moment
):
    slots_total = lax.axis_size("expert")
    width_dev = weight.shape[1]
    hidden = weight.shape[2]
    limit = 4.0 * math.sqrt(slots_total // 2 * width_dev * lax.axis_size("mp") * hidden)
    piece_len = width_dev * hidden // slots_total
    grads = local_grad(tokens[0], cotangent[0], counts[0])
    flat_grad = grads.reshape(slots_total, piece_len)
    flat_weight = weight.reshape(slots_total, piece_len)
    flat_first = first_moment.reshape(slots_total, piece_len)
    flat_second = second_moment.reshape(slots_total, piece_len)
    equal = place_now[None, :] == place_next[:, None]
    lowest = jnp.argmax(equal, axis=1)
    source = jnp.where(place_now == place_next, jnp.arange(slots_total, dtype=jnp.int32), lowest)
    spread_grad = lax.all_to_all(flat_grad, "expert", split_axis=0, concat_axis=0, tiled=True)
    paired = spread_grad + jnp.take(spread_grad, partner, axis=0)
    raw = lax.all_to_all(paired, "expert", split_axis=0, concat_axis=0, tiled=True)
    scale = clip_scale(0.5 * jnp.sum(raw * raw), limit)
    own_weight, own_first, own_second = adam_update(
        scale * raw, flat_weight, flat_first, flat_second
    )
    updated, first_new, second_new = (
        lax.all_to_all(own_weight, "expert", split_axis=0, concat_axis=0, tiled=True),
        lax.all_to_all(own_first, "expert", split_axis=0, concat_axis=0, tiled=True),
        lax.all_to_all(own_second, "expert", split_axis=0, concat_axis=0, tiled=True),
    )
    chosen = (
        jnp.take(updated, source, axis=0),
        jnp.take(first_new, source, axis=0),
        jnp.take(second_new, source, axis=0),
    )
    out_weight, out_first, out_second = relay_back(chosen)
    shape = weight.shape
    return (out_weight.reshape(shape), out_first.reshape(shape), out_second.reshape(shape))


def solution(mesh):
    placed = (
        P("expert", None, "mp"),
        P("expert", None, None),
        P("expert"),
        P(),
        P(),
        P(),
        P("expert", "mp", None),
        P("expert", "mp", None),
        P("expert", "mp", None),
    )
    return jax.shard_map(
        on_device,
        mesh=mesh,
        in_specs=placed,
        out_specs=(P("expert", "mp", None), P("expert", "mp", None), P("expert", "mp", None)),
        check_vma=False,
    )
```

profile of v0, /device:TPU:1, one launch (start us, length us, event | category | flops | bytes accessed | tf_op | source)
XLA Modules:
  0.0 500.7 jit_solution(7508422534748508622)
XLA Ops:
  2.5 3.3 fusion.2
  7.7 2.7 all_to_all.67
  10.4 13.1 %all-to-all-start = ((f32[64,1,6144]{2,1,0:T(1,128)}), f32[64,1,6144]{2,1,0:T(1,128)S(1)}, u32[]{:S(2)}, u32[]{:S(2)}) async-start(f32[64,1,6144]{2,1,0:T(1,128)} %all_to_all.67), calls=%async_computation | async-start | bytes 3145728 | tf_op jit(solution)/shard_map/all_to_all | solution.py:52
  23.6 38.9 %all-to-all-done = f32[64,1,6144]{2,1,0:T(1,128)S(1)} async-done(((f32[64,1,6144]{2,1,0:T(1,128)}), f32[64,1,6144]{2,1,0:T(1,128)S(1)}, u32[]{:S(2)}, u32[]{:S(2)}) %all-to-all-start) | async-done | bytes 1572896 | tf_op jit(solution)/shard_map/all_to_all | solution.py:52
  67.2 2.8 copy.27
  70.0 6.5 %all-to-all-start.1 = ((f32[64,1,6144]{2,1,0:T(1,128)}), f32[64,1,6144]{2,1,0:T(1,128)S(1)}, u32[]{:S(2)}, u32[]{:S(2)}) async-start(f32[64,1,6144]{2,1,0:T(1,128)} %copy.27), calls=%async_computation.1 | async-start | bytes 3145728 | tf_op jit(solution)/shard_map/all_to_all | solution.py:54
  82.3 33.1 %all-to-all-done.1 = f32[64,1,6144]{2,1,0:T(1,128)S(1)} async-done(((f32[64,1,6144]{2,1,0:T(1,128)}), f32[64,1,6144]{2,1,0:T(1,128)S(1)}, u32[]{:S(2)}, u32[]{:S(2)}) %all-to-all-start.1) | async-done | bytes 1572896 | tf_op jit(solution)/shard_map/all_to_all | solution.py:54
  115.5 3.8 multiply_reduce_fusion
  122.7 76.2 %psum.7 = f32[]{:T(128)} all-reduce(f32[]{:T(128)S(6)} %mul_shard_map.3), channel_id=1, replica_groups=mesh['expert'=64,'mp'=4] {'expert','mp'}, use_global_device_ids=true, to_apply=%region_1.3 | all-reduce | flops 1 | bytes 8 | tf_op jit(solution)/shard_map/psum | solution.py:17
  199.6 4.9 multiply_subtract_fusion
  204.5 2.8 copy.29
  207.2 6.1 %all-to-all-start.2 = ((f32[64,1,6144]{2,1,0:T(1,128)}), f32[64,1,6144]{2,1,0:T(1,128)S(1)}, u32[]{:S(2)}, u32[]{:S(2)}) async-start(f32[64,1,6144]{2,1,0:T(1,128)} %copy.29), calls=%async_computation.2 | async-start | bytes 3145728 | tf_op jit(solution)/shard_map/all_to_all | solution.py:60
  213.4 2.8 copy.31
  216.2 36.2 %all-to-all-done.2 = f32[64,1,6144]{2,1,0:T(1,128)S(1)} async-done(((f32[64,1,6144]{2,1,0:T(1,128)}), f32[64,1,6144]{2,1,0:T(1,128)S(1)}, u32[]{:S(2)}, u32[]{:S(2)}) %all-to-all-start.2) | async-done | bytes 1572896 | tf_op jit(solution)/shard_map/all_to_all | solution.py:60
  252.4 6.5 %all-to-all-start.4 = ((f32[64,1,6144]{2,1,0:T(1,128)}), f32[64,1,6144]{2,1,0:T(1,128)S(1)}, u32[]{:S(2)}, u32[]{:S(2)}) async-start(f32[64,1,6144]{2,1,0:T(1,128)} %copy.31), calls=%async_computation.4 | async-start | bytes 3145728 | tf_op jit(solution)/shard_map/all_to_all | solution.py:61
  258.9 4.2 copy.33
  263.0 34.8 %all-to-all-done.4 = f32[64,1,6144]{2,1,0:T(1,128)S(1)} async-done(((f32[64,1,6144]{2,1,0:T(1,128)}), f32[64,1,6144]{2,1,0:T(1,128)S(1)}, u32[]{:S(2)}, u32[]{:S(2)}) %all-to-all-start.4) | async-done | bytes 1572896 | tf_op jit(solution)/shard_map/all_to_all | solution.py:61
  299.0 7.0 %all-to-all-start.6 = ((f32[64,1,6144]{2,1,0:T(1,128)}), f32[64,1,6144]{2,1,0:T(1,128)}, u32[]{:S(2)}, u32[]{:S(2)}) async-start(f32[64,1,6144]{2,1,0:T(1,128)} %copy.33), calls=%async_computation.6 | async-start | bytes 3145728 | tf_op jit(solution)/shard_map/all_to_all | solution.py:62
  312.1 32.7 %all-to-all-done.6 = f32[64,1,6144]{2,1,0:T(1,128)} async-done(((f32[64,1,6144]{2,1,0:T(1,128)}), f32[64,1,6144]{2,1,0:T(1,128)}, u32[]{:S(2)}, u32[]{:S(2)}) %all-to-all-start.6) | async-done | bytes 1572896 | tf_op jit(solution)/shard_map/all_to_all | solution.py:62
  348.8 2.9 select_bitcast_fusion
  351.8 2.8 copy.34
  354.5 6.6 %all-to-all-start.7 = ((f32[64,1,6144]{2,1,0:T(1,128)}), f32[64,1,6144]{2,1,0:T(1,128)}, u32[]{:S(2)}, u32[]{:S(2)}) async-start(f32[64,1,6144]{2,1,0:T(1,128)} %copy.34), calls=%async_computation.7 | async-start | bytes 3145728 | tf_op jit(solution)/shard_map/all_to_all | solution.py:32
  361.2 2.8 copy.30
  364.0 36.2 %all-to-all-done.7 = f32[64,1,6144]{2,1,0:T(1,128)} async-done(((f32[64,1,6144]{2,1,0:T(1,128)}), f32[64,1,6144]{2,1,0:T(1,128)}, u32[]{:S(2)}, u32[]{:S(2)}) %all-to-all-start.7) | async-done | bytes 1572896 | tf_op jit(solution)/shard_map/all_to_all | solution.py:32
  400.1 6.5 %all-to-all-start.3 = ((f32[64,1,6144]{2,1,0:T(1,128)}), f32[64,1,6144]{2,1,0:T(1,128)S(1)}, u32[]{:S(2)}, u32[]{:S(2)}) async-start(f32[64,1,6144]{2,1,0:T(1,128)} %copy.30), calls=%async_computation.3 | async-start | bytes 3145728 | tf_op jit(solution)/shard_map/all_to_all | solution.py:30
  406.6 2.8 copy.32
  409.4 36.2 %all-to-all-done.3 = f32[64,1,6144]{2,1,0:T(1,128)S(1)} async-done(((f32[64,1,6144]{2,1,0:T(1,128)}), f32[64,1,6144]{2,1,0:T(1,128)S(1)}, u32[]{:S(2)}, u32[]{:S(2)}) %all-to-all-start.3) | async-done | bytes 1572896 | tf_op jit(solution)/shard_map/all_to_all | solution.py:30
  445.6 6.9 %all-to-all-start.5 = ((f32[64,1,6144]{2,1,0:T(1,128)}), f32[64,1,6144]{2,1,0:T(1,128)}, u32[]{:S(2)}, u32[]{:S(2)}) async-start(f32[64,1,6144]{2,1,0:T(1,128)} %copy.32), calls=%async_computation.5 | async-start | bytes 3145728 | tf_op jit(solution)/shard_map/all_to_all | solution.py:31
  452.5 5.1 %reduce.21 = f32[64,6144]{1,0:T(8,128)S(1)} reduce(f32[64,1,6144]{2,1,0:T(1,128)} %all-to-all-done.7, f32[]{:T(128)} %constant.52), dimensions={1}, to_apply=%all_to_all.66.reduce_sub_computation | reduce | bytes 3145732 | tf_op jit(solution)/shard_map/all_to_all | solution.py:32
  459.0 3.7 reduce.19
  464.1 27.0 %all-to-all-done.5 = f32[64,1,6144]{2,1,0:T(1,128)} async-done(((f32[64,1,6144]{2,1,0:T(1,128)}), f32[64,1,6144]{2,1,0:T(1,128)}, u32[]{:S(2)}, u32[]{:S(2)}) %all-to-all-start.5) | async-done | bytes 1572896 | tf_op jit(solution)/shard_map/all_to_all | solution.py:31
  491.2 6.5 %reduce.20 = f32[64,6144]{1,0:T(8,128)} reduce(f32[64,1,6144]{2,1,0:T(1,128)} %all-to-all-done.5, f32[]{:T(128)} %constant.52), dimensions={1}, to_apply=%all_to_all.62.reduce_sub_computation | reduce | bytes 3145732 | tf_op jit(solution)/shard_map/all_to_all | solution.py:31
  (43 shorter events, 32.8 us)
Async XLA Ops:
  0.6 1.9 copy-start
  10.4 13.1 %copy-start.8 = (s32[64]{0:T(128)S(1)}, s32[64]{0:T(128)}, u32[]{:S(2)}) copy-start(s32[64]{0:T(128)} %param.15) | copy-start | bytes 772
  10.4 52.1 %all-to-all-start = ((f32[64,1,6144]{2,1,0:T(1,128)}), f32[64,1,6144]{2,1,0:T(1,128)S(1)}, u32[]{:S(2)}, u32[]{:S(2)}) async-start(f32[64,1,6144]{2,1,0:T(1,128)} %all_to_all.67), calls=%async_computation | async-start | bytes 3145728 | tf_op jit(solution)/shard_map/all_to_all | solution.py:52
  70.0 45.5 %all-to-all-start.1 = ((f32[64,1,6144]{2,1,0:T(1,128)}), f32[64,1,6144]{2,1,0:T(1,128)S(1)}, u32[]{:S(2)}, u32[]{:S(2)}) async-start(f32[64,1,6144]{2,1,0:T(1,128)} %copy.27), calls=%async_computation.1 | async-start | bytes 3145728 | tf_op jit(solution)/shard_map/all_to_all | solution.py:54
  119.9 79.6 %copy-start.4 = (f32[64,1,6144]{2,0,1:T(8,128)S(1)}, f32[64,1,6144]{2,0,1:T(8,128)}, u32[]{:S(2)}) copy-start(f32[64,1,6144]{2,0,1:T(8,128)} %mul.84) | copy-start | bytes 4718596
  207.2 6.2 %copy-start.5 = (f32[64,1,6144]{2,0,1:T(8,128)S(1)}, f32[64,1,6144]{2,0,1:T(8,128)}, u32[]{:S(2)}) copy-start(f32[64,1,6144]{2,0,1:T(8,128)} %get-tuple-element.9) | copy-start | bytes 4718596
  207.2 45.1 %all-to-all-start.2 = ((f32[64,1,6144]{2,1,0:T(1,128)}), f32[64,1,6144]{2,1,0:T(1,128)S(1)}, u32[]{:S(2)}, u32[]{:S(2)}) async-start(f32[64,1,6144]{2,1,0:T(1,128)} %copy.29), calls=%async_computation.2 | async-start | bytes 3145728 | tf_op jit(solution)/shard_map/all_to_all | solution.py:60
  252.4 45.5 %all-to-all-start.4 = ((f32[64,1,6144]{2,1,0:T(1,128)}), f32[64,1,6144]{2,1,0:T(1,128)S(1)}, u32[]{:S(2)}, u32[]{:S(2)}) async-start(f32[64,1,6144]{2,1,0:T(1,128)} %copy.31), calls=%async_computation.4 | async-start | bytes 3145728 | tf_op jit(solution)/shard_map/all_to_all | solution.py:61
  263.0 43.0 %copy-start.6 = (s32[64]{0:T(128)S(1)}, s32[64]{0:T(128)}, u32[]{:S(2)}) copy-start(s32[64]{0:T(128)} %param.14) | copy-start | bytes 772
  263.0 43.0 %copy-start.7 = (s32[64]{0:T(128)S(1)}, s32[64]{0:T(128)}, u32[]{:S(2)}) copy-start(s32[64]{0:T(128)} %param.16) | copy-start | bytes 772
  297.9 1.1 copy-start.2
  299.0 45.8 %all-to-all-start.6 = ((f32[64,1,6144]{2,1,0:T(1,128)}), f32[64,1,6144]{2,1,0:T(1,128)}, u32[]{:S(2)}, u32[]{:S(2)}) async-start(f32[64,1,6144]{2,1,0:T(1,128)} %copy.33), calls=%async_computation.6 | async-start | bytes 3145728 | tf_op jit(solution)/shard_map/all_to_all | solution.py:62
  307.3 2.2 copy-start.3
  354.5 45.6 %all-to-all-start.7 = ((f32[64,1,6144]{2,1,0:T(1,128)}), f32[64,1,6144]{2,1,0:T(1,128)}, u32[]{:S(2)}, u32[]{:S(2)}) async-start(f32[64,1,6144]{2,1,0:T(1,128)} %copy.34), calls=%async_computation.7 | async-start | bytes 3145728 | tf_op jit(solution)/shard_map/all_to_all | solution.py:32
  400.1 45.5 %all-to-all-start.3 = ((f32[64,1,6144]{2,1,0:T(1,128)}), f32[64,1,6144]{2,1,0:T(1,128)S(1)}, u32[]{:S(2)}, u32[]{:S(2)}) async-start(f32[64,1,6144]{2,1,0:T(1,128)} %copy.30), calls=%async_computation.3 | async-start | bytes 3145728 | tf_op jit(solution)/shard_map/all_to_all | solution.py:30
  445.6 45.6 %all-to-all-start.5 = ((f32[64,1,6144]{2,1,0:T(1,128)}), f32[64,1,6144]{2,1,0:T(1,128)}, u32[]{:S(2)}, u32[]{:S(2)}) async-start(f32[64,1,6144]{2,1,0:T(1,128)} %copy.32), calls=%async_computation.5 | async-start | bytes 3145728 | tf_op jit(solution)/shard_map/all_to_all | solution.py:31
  491.2 9.1 %copy-start.1 = (bf16[1,1024,1536]{2,1,0:T(8,128)(2,1)S(1)}, bf16[1,1024,1536]{2,1,0:T(8,128)(2,1)}, u32[]{:S(2)}) copy-start(bf16[1,1024,1536]{2,1,0:T(8,128)(2,1)} %param.11) | copy-start | bytes 9437188
where the time goes:
time: 510 us; the launch traced here: 501 us
  waiting for transfers between devices  275 us (54%)
  blocking collectives  76.2 us (15%)
  starting transfers between devices  59.2 us (12%)
  local copies, waits for them, and re-layouts  50.4 us (10%)
  other arithmetic  32.8 us (6%)
    psum x1, blocking collectives, clip_scale(): sumsq = lax.psum(partial_sum, ('expert', 'mp'))  76.2 us
    all_to_all x1, waiting for transfers between devices, on_device(): lax.all_to_all(flat_grad, 'expert', split_axis=0, concat_axis=0, tiled=True)  38.9 us
    all_to_all x1, waiting for transfers between devices, relay_back(): lax.all_to_all(states[0], 'expert', split_axis=0, concat_axis=0, tiled=True)  36.2 us
    all_to_all x1, waiting for transfers between devices, on_device(): lax.all_to_all(own_weight, 'expert', split_axis=0, concat_axis=0, tiled=T...  36.2 us
    all_to_all x1, waiting for transfers between devices, relay_back(): lax.all_to_all(states[2], 'expert', split_axis=0, concat_axis=0, tiled=True)  36.2 us
    all_to_all x1, waiting for transfers between devices, on_device(): lax.all_to_all(own_first, 'expert', split_axis=0, concat_axis=0, tiled=True)  34.8 us
    all_to_all x1, waiting for transfers between devices, on_device(): lax.all_to_all(paired, 'expert', split_axis=0, concat_axis=0, tiled=True)  33.1 us
    all_to_all x1, waiting for transfers between devices, on_device(): lax.all_to_all(own_second, 'expert', split_axis=0, concat_axis=0, tiled=T...  32.7 us
  transfers between devices with their start and end apart: 8, of which 8 were waited for; matrix products, arithmetic and copies ran while one was open for 7% of the time, Pallas kernels for 0%

commit v1 on v0

v1 whole, which is shorter than its diff:
```python
import functools
import math

import jax
import jax.numpy as jnp
from jax import lax
from jax.experimental import pallas as pl
from jax.experimental.pallas import tpu as pltpu
from jax.sharding import PartitionSpec as P

LANES = 128


def local_grad(block, grad_rows, live):
    rows_total = block.shape[0]
    row_ids = jnp.arange(rows_total, dtype=jnp.int32)
    masked = jnp.where((row_ids < live)[:, None], grad_rows, jnp.zeros_like(grad_rows))
    return jnp.einsum("rd,rh->dh", block, masked, preferred_element_type=jnp.float32)


def sumsq_kernel(slots, partner_ref, grad_ref, out_ref):
    def body(slot, acc):
        raw = grad_ref[slot] + grad_ref[partner_ref[slot]]
        return acc + raw * raw

    zero = jnp.zeros(grad_ref.shape[1:], jnp.float32)
    acc = lax.fori_loop(0, slots, body, zero, unroll=4)
    rows, cols = acc.shape
    part = sum(
        acc[r : r + 8, c : c + LANES] for r in range(0, rows, 8) for c in range(0, cols, LANES)
    )
    out_ref[...] = jnp.broadcast_to(0.5 * jnp.sum(part), out_ref.shape)


def update_kernel(
    slots, limit, source_ref, partner_ref, sum_ref, grad_ref, state_ref, out_ref
):
    clip = jnp.minimum(jnp.float32(1.0), limit / jnp.sqrt(sum_ref[...] + 1e-06))

    def update(slot, carry):
        source = source_ref[slot]
        other = partner_ref[source]
        for start in range(0, grad_ref.shape[2], LANES):
            cols = pl.ds(start, LANES)
            total = clip * (grad_ref[source, :, cols] + grad_ref[other, :, cols])
            weight = state_ref[source, 0, :, cols]
            first = 0.9 * state_ref[source, 1, :, cols] + 0.1 * total
            second = 0.95 * state_ref[source, 2, :, cols] + 0.05 * total * total
            step = (first / (1.0 - 0.9**10)) / (jnp.sqrt(second / (1.0 - 0.95**10)) + 1e-08)
            out_ref[slot, 0, :, cols] = weight - 0.1 * (step + 0.3 * weight)
            out_ref[slot, 1, :, cols] = first
            out_ref[slot, 2, :, cols] = second
        return carry

    lax.fori_loop(0, slots, update, 0, unroll=4)


def shifted(value, axis, pairs_of):
    total = value
    for pairs in pairs_of:
        total = total + lax.ppermute(value, axis, pairs)
    return total


def all_sum(value):
    slots = lax.axis_size("expert")
    width = lax.axis_size("mp")
    inner = 8
    outer = slots // inner
    value = shifted(
        value, "mp", [[(i, (i + k) % width) for i in range(width)] for k in range(1, width)]
    )
    value = shifted(
        value, "expert", [[(i, i ^ k) for i in range(slots)] for k in range(1, inner)]
    )
    return shifted(
        value,
        "expert",
        [[(i, (i + k * inner) % slots) for i in range(slots)] for k in range(1, outer)],
    )


def on_device(
    tokens, cotangent, counts, place_now, partner, place_next, weight, first_moment, second_moment
):
    slots = lax.axis_size("expert")
    units = slots // 2
    width_dev = weight.shape[1]
    hidden = weight.shape[2]
    rows = width_dev // slots
    limit = 4.0 * math.sqrt(units * width_dev * lax.axis_size("mp") * hidden)

    equal = place_now[None, :] == place_next[:, None]
    lowest = jnp.argmax(equal, axis=1).astype(jnp.int32)
    source = jnp.where(place_now == place_next, jnp.arange(slots, dtype=jnp.int32), lowest)

    grads = local_grad(tokens[0], cotangent[0], counts[0]).reshape(slots, rows, hidden)
    states = jnp.stack(
        [array.reshape(slots, rows, hidden) for array in (weight, first_moment, second_moment)],
        axis=1,
    )
    spread = lax.all_to_all(grads, "expert", split_axis=0, concat_axis=0, tiled=True)
    spread, states = lax.optimization_barrier((spread, states))
    states = lax.all_to_all(states, "expert", split_axis=0, concat_axis=0, tiled=True)

    smem = pl.BlockSpec(memory_space=pltpu.SMEM)
    part = pl.pallas_call(
        functools.partial(sumsq_kernel, slots),
        out_shape=jax.ShapeDtypeStruct((8, LANES), jnp.float32),
        in_specs=[smem, pl.BlockSpec(memory_space=pltpu.VMEM)],
        out_specs=pl.BlockSpec(memory_space=pltpu.VMEM),
        cost_estimate=pl.CostEstimate(
            flops=spread.size, bytes_accessed=spread.size * 4, transcendentals=0
        ),
    )(partner, spread)
    sumsq = all_sum(part)

    chunk = 8
    out = pl.pallas_call(
        functools.partial(update_kernel, slots, limit),
        grid=(rows // chunk,),
        out_shape=jax.ShapeDtypeStruct((slots, 3, rows, hidden), jnp.float32),
        in_specs=[
            smem,
            smem,
            pl.BlockSpec((8, LANES), lambda i: (0, 0)),
            pl.BlockSpec((slots, chunk, hidden), lambda i: (0, i, 0)),
            pl.BlockSpec((slots, 3, chunk, hidden), lambda i: (0, 0, i, 0)),
        ],
        out_specs=pl.BlockSpec((slots, 3, chunk, hidden), lambda i: (0, 0, i, 0)),
        compiler_params=pltpu.CompilerParams(vmem_limit_bytes=32 * 2**20),
    )(source, partner, sumsq, spread, states)
    out = lax.all_to_all(out, "expert", split_axis=0, concat_axis=0, tiled=True)
    return tuple(out[:, k].reshape(weight.shape) for k in range(3))


def solution(mesh):
    placed = (
        P("expert", None, "mp"),
        P("expert", None, None),
        P("expert"),
        P(),
        P(),
        P(),
        P("expert", "mp", None),
        P("expert", "mp", None),
        P("expert", "mp", None),
    )
    return jax.shard_map(
        on_device,
        mesh=mesh,
        in_specs=placed,
        out_specs=(P("expert", "mp", None), P("expert", "mp", None), P("expert", "mp", None)),
        check_vma=False,
    )
```

time: 510 us -> 301 us (0.59); the launches traced: 501 us -> 300 us
  waiting for transfers between devices: 275 us -> 109 us
  local copies, waits for them, and re-layouts: 50.4 us -> 6.42 us
  blocking collectives: 76.2 us -> 117 us
  other arithmetic: 32.8 us -> 6.28 us
  starting transfers between devices: 59.2 us -> 49.2 us
  Pallas kernels: 0 us -> 7.29 us
    all_to_all x8 -> x2, waiting for transfers between devices: 275 us -> 34.1 us  [the longest x1 34.1 us: on_device(): lax.all_to_all(grads, 'expert', split_axis=0, concat_axis=0, tiled=True)]
    all_to_all x0 -> x1, blocking collectives: none -> 117 us  [on_device(): out = lax.all_to_all(out, 'expert', split_axis=0, concat_axis=0, tiled=True)]
    psum x1 -> x0, blocking collectives: 76.2 us -> none  [clip_scale(): sumsq = lax.psum(partial_sum, ('expert', 'mp'))]
    ppermute x0 -> x17, waiting for transfers between devices: none -> 74.8 us  [shifted(): total = total + lax.ppermute(value, axis, pairs)]
    all_to_all x8 -> x2, starting transfers between devices: 59.2 us -> 19.8 us  [the longest x1 13.2 us: on_device(): lax.all_to_all(grads, 'expert', split_axis=0, concat_axis=0, tiled=True)]
    ppermute x0 -> x17, starting transfers between devices: none -> 29.4 us  [shifted(): total = total + lax.ppermute(value, axis, pairs)]
    all_to_all x5 -> x0, other arithmetic: 20.3 us -> none  [the longest x2 8.09 us: relay_back(): lax.all_to_all(states[2], 'expert', split_axis=0, concat_axis=0, tiled=True)]
    all_to_all x5 -> x0, local copies, waits for them, and re-layouts: 13.8 us -> none  [the longest x1 2.76 us: relay_back(): lax.all_to_all(states[2], 'expert', split_axis=0, concat_axis=0, tiled=True)]
  transfers between devices with their start and end apart: 8 -> 19, of which waited for: 8 -> 8; matrix products, arithmetic and copies ran while one was open for 7% -> 2% of each run, Pallas kernels for 0% -> 1%
where the time goes in v1:
time: 301 us; the launch traced here: 300 us
  blocking collectives  117 us (39%)
  waiting for transfers between devices  109 us (36%)
  starting transfers between devices  49.2 us (16%)
  Pallas kernels  7.29 us (2%)
  local copies, waits for them, and re-layouts  6.42 us (2%)
  other arithmetic  6.28 us (2%)
  matrix products  3.28 us (1%)
    all_to_all x1, blocking collectives, on_device(): out = lax.all_to_all(out, 'expert', split_axis=0, concat_axis=0, tiled=True)  117 us
    ppermute x17, waiting for transfers between devices, shifted(): total = total + lax.ppermute(value, axis, pairs)  74.8 us
    all_to_all x1, waiting for transfers between devices, on_device(): lax.all_to_all(grads, 'expert', split_axis=0, concat_axis=0, tiled=True)  34.1 us
    ppermute x17, starting transfers between devices, shifted(): total = total + lax.ppermute(value, axis, pairs)  29.4 us
    all_to_all x1, starting transfers between devices, on_device(): lax.all_to_all(grads, 'expert', split_axis=0, concat_axis=0, tiled=True)  13.2 us
    all_to_all x1, starting transfers between devices, on_device(): lax.all_to_all(states, 'expert', split_axis=0, concat_axis=0, tiled=True)  6.63 us
  transfers between devices with their start and end apart: 19, of which 8 were waited for; matrix products, arithmetic and copies ran while one was open for 2% of the time, Pallas kernels for 1%

profile of v1, /device:TPU:1, one launch (start us, length us, event | category | flops | bytes accessed | tf_op | source)
XLA Modules:
  0.0 300.3 jit_solution(14761427119217807537)
XLA Ops:
  1.5 1.1 copy-done
  2.5 3.3 %fusion.2 = f32[1536,256]{0,1:T(8,128)} fusion(bf16[1,1024,1536]{2,1,0:T(8,128)(2,1)S(1)} %copy-done, bf16[1,1024,256]{2,1,0:T(8,128)(2,1)} %param.10, pred[1024]{0:T(1024)(128)(4,1)S(1)} %iota_compare_fusion), kind=kOutput, calls=%fused_computation.3 | convolution fusion | flops 805568512 | bytes 5243904 | tf_op jit(solution)/shard_map/rd,rh->dh/dot_general | solution.py:18
  5.8 3.0 %copy.13 = f32[1536,256]{1,0:T(8,128)} copy(f32[1536,256]{0,1:T(8,128)} %fusion.2) | data formatting | bytes 3145728 | tf_op jit(solution)/shard_map/rd,rh->dh/dot_general | solution.py:18
  8.8 13.2 %all-to-all-start = ((f32[64,24,256]{2,1,0:T(8,128)}), f32[64,24,256]{2,1,0:T(8,128)}, u32[]{:S(2)}, u32[]{:S(2)}) async-start(f32[64,24,256]{2,1,0:T(8,128)} %bitcast.19), calls=%async_computation | async-start | bytes 3145728 | tf_op jit(solution)/shard_map/all_to_all | solution.py:102
  22.0 4.9 %pad_maximum_fusion = f32[64,3,24,256]{3,2,1,0:T(8,128)} fusion(f32[64,1,24,256]{3,2,1,0:T(8,128)} %bitcast.20, f32[64,1,24,256]{3,2,1,0:T(8,128)} %bitcast.21, f32[64,1,24,256]{3,2,1,0:T(8,128)} %bitcast.22), kind=kLoop, calls=%fused_computation | loop fusion | flops 2359296 | bytes 9437184 | tf_op jit(solution)/shard_map/stack | solution.py:98
  26.9 34.1 %all-to-all-done.grad_ref = f32[64,24,256]{2,1,0:T(8,128)} async-done(((f32[64,24,256]{2,1,0:T(8,128)}), f32[64,24,256]{2,1,0:T(8,128)}, u32[]{:S(2)}, u32[]{:S(2)}) %all-to-all-start) | async-done | bytes 1572896 | tf_op jit(solution)/shard_map/all_to_all | solution.py:102
  60.9 6.6 %all-to-all-start.1 = ((f32[64,3,24,256]{3,2,1,0:T(8,128)}), f32[64,3,24,256]{3,2,1,0:T(8,128)}, u32[]{:S(2)}, u32[]{:S(2)}) async-start(f32[64,3,24,256]{3,2,1,0:T(8,128)} %pad_maximum_fusion), calls=%async_computation.1 | async-start | bytes 9437184 | tf_op jit(solution)/shard_map/all_to_all | solution.py:104
  67.6 2.4 shard_map.112
  70.0 1.3 collective-permute-start
  71.3 2.6 collective-permute-start.1
  74.0 1.1 collective-permute-start.2
  75.0 0.9 collective-permute-done.1
  75.9 1.1 collective-permute-done.2
  77.7 1.9 collective-permute-start.3
  79.7 1.1 collective-permute-start.4
  81.3 2.6 collective-permute-start.6
  84.7 2.4 collective-permute-start.8
  87.5 1.1 collective-permute-done.7
  88.6 3.1 %collective-permute-done.9 = f32[8,128]{1,0:T(8,128)S(1)} collective-permute-done((f32[8,128]{1,0:T(8,128)S(1)}, f32[8,128]{1,0:T(8,128)S(1)}, u32[]{:S(2)}, u32[]{:S(2)}) %collective-permute-start.9) | collective-permute-done | bytes 4128 | tf_op jit(solution)/shard_map/ppermute | solution.py:61
  91.7 1.3 collective-permute-start.10
  93.0 2.2 collective-permute-start.11
  95.9 2.6 collective-permute-start.12
  98.5 1.8 collective-permute-start.13
  100.3 2.7 collective-permute-start.14
  103.0 64.9 %collective-permute-done.10 = f32[8,128]{1,0:T(8,128)S(1)} collective-permute-done((f32[8,128]{1,0:T(8,128)S(1)}, f32[8,128]{1,0:T(8,128)S(1)}, u32[]{:S(2)}, u32[]{:S(2)}) %collective-permute-start.10) | collective-permute-done | bytes 4128 | tf_op jit(solution)/shard_map/ppermute | solution.py:61
  167.9 3.3 %collective-permute-start.15 = (f32[8,128]{1,0:T(8,128)S(1)}, f32[8,128]{1,0:T(8,128)S(1)}, u32[]{:S(2)}, u32[]{:S(2)}) collective-permute-start(f32[8,128]{1,0:T(8,128)S(1)} %add_add_fusion.1), channel_id=1, source_target_pairs={{0,192},{4,196},{8,200},{12,204},{16,208},{20,212},{24,216},{28,22... | collective-permute-start | bytes 12296 | tf_op jit(solution)/shard_map/ppermute | solution.py:61
  171.2 1.7 collective-permute-done.11
  172.9 0.8 collective-permute-start.16
  173.8 1.9 collective-permute-done.16
  175.7 4.9 %shard_map.113 = f32[64,3,24,256]{3,2,1,0:T(8,128)S(1)} custom-call(s32[64]{0:T(128)S(1)} %compare_select_fusion.source_ref, s32[64]{0:T(128)S(1)} %copy-done.1, f32[8,128]{1,0:T(8,128)S(1)} %add_add_fusion.sum_ref, f32[64,24,256]{2,1,0:T(8,128)} %all-to-all-done.grad_ref, f32[64,3,24,256]{3,2,1,0:T(8,128)} %all-to-all-done.1.state_ref), custom_call_target="tpu_custom_call" | custom-call | tf_op jit(solution)/shard_map/pallas_call | solution.py:119
  180.6 117.4 %all_to_all.15 = f32[64,3,24,256]{3,2,1,0:T(8,128)S(1)} all-to-all(f32[64,3,24,256]{3,2,1,0:T(8,128)S(1)} %shard_map.113), channel_id=1, replica_groups=mesh['expert'=64,'mp'=4] {'expert'}, dimensions={0} | all-to-all | bytes 9437184 | tf_op jit(solution)/shard_map/all_to_all | solution.py:133
  298.0 2.3 fusion.10
  (27 shorter events, 3.2 us)
Async XLA Ops:
  0.6 1.9 copy-start
  8.8 52.1 %all-to-all-start = ((f32[64,24,256]{2,1,0:T(8,128)}), f32[64,24,256]{2,1,0:T(8,128)}, u32[]{:S(2)}, u32[]{:S(2)}) async-start(f32[64,24,256]{2,1,0:T(8,128)} %bitcast.19), calls=%async_computation | async-start | bytes 3145728 | tf_op jit(solution)/shard_map/all_to_all | solution.py:102
  60.9 114.8 %all-to-all-start.1 = ((f32[64,3,24,256]{3,2,1,0:T(8,128)}), f32[64,3,24,256]{3,2,1,0:T(8,128)}, u32[]{:S(2)}, u32[]{:S(2)}) async-start(f32[64,3,24,256]{3,2,1,0:T(8,128)} %pad_maximum_fusion), calls=%async_computation.1 | async-start | bytes 9437184 | tf_op jit(solution)/shard_map/all_to_all | solution.py:104
  67.6 27.6 %copy-start.2 = (s32[64]{0:T(128)S(1)}, s32[64]{0:T(128)}, u32[]{:S(2)}) copy-start(s32[64]{0:T(128)} %param.12) | copy-start | bytes 772
  67.6 27.6 %copy-start.3 = (s32[64]{0:T(128)S(1)}, s32[64]{0:T(128)}, u32[]{:S(2)}) copy-start(s32[64]{0:T(128)} %param.14) | copy-start | bytes 772
  67.6 108.1 %copy-start.1 = (s32[64]{0:T(128)S(1)}, s32[64]{0:T(128)}, u32[]{:S(2)}) copy-start(s32[64]{0:T(128)} %partner_ref.3) | copy-start | bytes 772
  70.0 5.0 %collective-permute-start = (f32[8,128]{1,0:T(8,128)}, f32[8,128]{1,0:T(8,128)S(1)}, u32[]{:S(2)}, u32[]{:S(2)}) collective-permute-start(f32[8,128]{1,0:T(8,128)} %shard_map.112), channel_id=1, source_target_pairs={{0,1},{1,2},{2,3},{3,0},{4,5},{5,6},{6,7},{7,4},{8,9},{9,10},{10,1... | collective-permute-start | bytes 12296 | tf_op jit(solution)/shard_map/ppermute | solution.py:61
  71.3 4.6 %collective-permute-start.1 = (f32[8,128]{1,0:T(8,128)}, f32[8,128]{1,0:T(8,128)S(1)}, u32[]{:S(2)}, u32[]{:S(2)}) collective-permute-start(f32[8,128]{1,0:T(8,128)} %shard_map.112), channel_id=1, source_target_pairs={{0,2},{1,3},{2,0},{3,1},{4,6},{5,7},{6,4},{7,5},{8,10},{9,11},{10,... | collective-permute-start | bytes 12296 | tf_op jit(solution)/shard_map/ppermute | solution.py:61
  74.0 3.1 %collective-permute-start.2 = (f32[8,128]{1,0:T(8,128)}, f32[8,128]{1,0:T(8,128)S(1)}, u32[]{:S(2)}, u32[]{:S(2)}) collective-permute-start(f32[8,128]{1,0:T(8,128)} %shard_map.112), channel_id=1, source_target_pairs={{0,3},{1,0},{2,1},{3,2},{4,7},{5,4},{6,5},{7,6},{8,11},{9,8},{10,9... | collective-permute-start | bytes 12296 | tf_op jit(solution)/shard_map/ppermute | solution.py:61
  77.7 6.9 %collective-permute-start.3 = (f32[8,128]{1,0:T(8,128)S(1)}, f32[8,128]{1,0:T(8,128)S(1)}, u32[]{:S(2)}, u32[]{:S(2)}) collective-permute-start(f32[8,128]{1,0:T(8,128)S(1)} %add_add_fusion.2), channel_id=1, source_target_pairs={{0,4},{4,0},{8,12},{12,8},{16,20},{20,16},{24,28},{28,24},{32,36},... | collective-permute-start | bytes 12296 | tf_op jit(solution)/shard_map/ppermute | solution.py:61
  79.7 7.4 %collective-permute-start.4 = (f32[8,128]{1,0:T(8,128)S(1)}, f32[8,128]{1,0:T(8,128)S(1)}, u32[]{:S(2)}, u32[]{:S(2)}) collective-permute-start(f32[8,128]{1,0:T(8,128)S(1)} %add_add_fusion.2), channel_id=1, source_target_pairs={{0,8},{4,12},{8,0},{12,4},{16,24},{20,28},{24,16},{28,20},{32,40},... | collective-permute-start | bytes 12296 | tf_op jit(solution)/shard_map/ppermute | solution.py:61
  80.8 6.7 %collective-permute-start.5 = (f32[8,128]{1,0:T(8,128)S(1)}, f32[8,128]{1,0:T(8,128)S(1)}, u32[]{:S(2)}, u32[]{:S(2)}) collective-permute-start(f32[8,128]{1,0:T(8,128)S(1)} %add_add_fusion.2), channel_id=1, source_target_pairs={{0,12},{4,8},{8,4},{12,0},{16,28},{20,24},{24,20},{28,16},{32,44},... | collective-permute-start | bytes 12296 | tf_op jit(solution)/shard_map/ppermute | solution.py:61
  81.3 6.2 %collective-permute-start.6 = (f32[8,128]{1,0:T(8,128)S(1)}, f32[8,128]{1,0:T(8,128)S(1)}, u32[]{:S(2)}, u32[]{:S(2)}) collective-permute-start(f32[8,128]{1,0:T(8,128)S(1)} %add_add_fusion.2), channel_id=1, source_target_pairs={{0,16},{4,20},{8,24},{12,28},{16,0},{20,4},{24,8},{28,12},{32,48},... | collective-permute-start | bytes 12296 | tf_op jit(solution)/shard_map/ppermute | solution.py:61
  83.9 4.6 %collective-permute-start.7 = (f32[8,128]{1,0:T(8,128)S(1)}, f32[8,128]{1,0:T(8,128)S(1)}, u32[]{:S(2)}, u32[]{:S(2)}) collective-permute-start(f32[8,128]{1,0:T(8,128)S(1)} %add_add_fusion.2), channel_id=1, source_target_pairs={{0,20},{4,16},{8,28},{12,24},{16,4},{20,0},{24,12},{28,8},{32,52},... | collective-permute-start | bytes 12296 | tf_op jit(solution)/shard_map/ppermute | solution.py:61
  84.7 3.9 %collective-permute-start.8 = (f32[8,128]{1,0:T(8,128)S(1)}, f32[8,128]{1,0:T(8,128)S(1)}, u32[]{:S(2)}, u32[]{:S(2)}) collective-permute-start(f32[8,128]{1,0:T(8,128)S(1)} %add_add_fusion.2), channel_id=1, source_target_pairs={{0,24},{4,28},{8,16},{12,20},{16,8},{20,12},{24,0},{28,4},{32,56},... | collective-permute-start | bytes 12296 | tf_op jit(solution)/shard_map/ppermute | solution.py:61
  87.0 4.7 %collective-permute-start.9 = (f32[8,128]{1,0:T(8,128)S(1)}, f32[8,128]{1,0:T(8,128)S(1)}, u32[]{:S(2)}, u32[]{:S(2)}) collective-permute-start(f32[8,128]{1,0:T(8,128)S(1)} %add_add_fusion.2), channel_id=1, source_target_pairs={{0,28},{4,24},{8,20},{12,16},{16,12},{20,8},{24,4},{28,0},{32,60},... | collective-permute-start | bytes 12296 | tf_op jit(solution)/shard_map/ppermute | solution.py:61
  91.7 76.2 %collective-permute-start.10 = (f32[8,128]{1,0:T(8,128)S(1)}, f32[8,128]{1,0:T(8,128)S(1)}, u32[]{:S(2)}, u32[]{:S(2)}) collective-permute-start(f32[8,128]{1,0:T(8,128)S(1)} %add_add_fusion.1), channel_id=1, source_target_pairs={{0,32},{4,36},{8,40},{12,44},{16,48},{20,52},{24,56},{28,60},{32,6... | collective-permute-start | bytes 12296 | tf_op jit(solution)/shard_map/ppermute | solution.py:61
  93.0 80.0 %collective-permute-start.11 = (f32[8,128]{1,0:T(8,128)S(1)}, f32[8,128]{1,0:T(8,128)S(1)}, u32[]{:S(2)}, u32[]{:S(2)}) collective-permute-start(f32[8,128]{1,0:T(8,128)S(1)} %add_add_fusion.1), channel_id=1, source_target_pairs={{0,64},{4,68},{8,72},{12,76},{16,80},{20,84},{24,88},{28,92},{32,9... | collective-permute-start | bytes 12296 | tf_op jit(solution)/shard_map/ppermute | solution.py:61
  95.9 77.8 %collective-permute-start.12 = (f32[8,128]{1,0:T(8,128)S(1)}, f32[8,128]{1,0:T(8,128)S(1)}, u32[]{:S(2)}, u32[]{:S(2)}) collective-permute-start(f32[8,128]{1,0:T(8,128)S(1)} %add_add_fusion.1), channel_id=1, source_target_pairs={{0,96},{4,100},{8,104},{12,108},{16,112},{20,116},{24,120},{28,124... | collective-permute-start | bytes 12296 | tf_op jit(solution)/shard_map/ppermute | solution.py:61
  98.5 75.3 %collective-permute-start.13 = (f32[8,128]{1,0:T(8,128)S(1)}, f32[8,128]{1,0:T(8,128)S(1)}, u32[]{:S(2)}, u32[]{:S(2)}) collective-permute-start(f32[8,128]{1,0:T(8,128)S(1)} %add_add_fusion.1), channel_id=1, source_target_pairs={{0,128},{4,132},{8,136},{12,140},{16,144},{20,148},{24,152},{28,15... | collective-permute-start | bytes 12296 | tf_op jit(solution)/shard_map/ppermute | solution.py:61
  100.3 73.4 %collective-permute-start.14 = (f32[8,128]{1,0:T(8,128)S(1)}, f32[8,128]{1,0:T(8,128)S(1)}, u32[]{:S(2)}, u32[]{:S(2)}) collective-permute-start(f32[8,128]{1,0:T(8,128)S(1)} %add_add_fusion.1), channel_id=1, source_target_pairs={{0,160},{4,164},{8,168},{12,172},{16,176},{20,180},{24,184},{28,18... | collective-permute-start | bytes 12296 | tf_op jit(solution)/shard_map/ppermute | solution.py:61
  167.9 5.8 %collective-permute-start.15 = (f32[8,128]{1,0:T(8,128)S(1)}, f32[8,128]{1,0:T(8,128)S(1)}, u32[]{:S(2)}, u32[]{:S(2)}) collective-permute-start(f32[8,128]{1,0:T(8,128)S(1)} %add_add_fusion.1), channel_id=1, source_target_pairs={{0,192},{4,196},{8,200},{12,204},{16,208},{20,212},{24,216},{28,22... | collective-permute-start | bytes 12296 | tf_op jit(solution)/shard_map/ppermute | solution.py:61
  172.9 2.8 collective-permute-start.16

commit v2 on v1

--- a/solution.py
+++ b/solution.py
@@ -33,7 +33,16 @@
 
 
 def update_kernel(
-    slots, limit, source_ref, partner_ref, sum_ref, grad_ref, state_ref, out_ref
+    slots,
+    limit,
+    source_ref,
+    partner_ref,
+    sum_ref,
+    grad_ref,
+    weight_ref,
+    first_ref,
+    second_ref,
+    out_ref,
 ):
     clip = jnp.minimum(jnp.float32(1.0), limit / jnp.sqrt(sum_ref[...] + 1e-06))
 
@@ -43,16 +52,17 @@
         for start in range(0, grad_ref.shape[2], LANES):
             cols = pl.ds(start, LANES)
             total = clip * (grad_ref[source, :, cols] + grad_ref[other, :, cols])
-            weight = state_ref[source, 0, :, cols]
-            first = 0.9 * state_ref[source, 1, :, cols] + 0.1 * total
-            second = 0.95 * state_ref[source, 2, :, cols] + 0.05 * total * total
-            step = (first / (1.0 - 0.9**10)) / (jnp.sqrt(second / (1.0 - 0.95**10)) + 1e-08)
+            weight = weight_ref[source, :, cols]
+            first = 0.9 * first_ref[source, :, cols] + 0.1 * total
+            second = 0.95 * second_ref[source, :, cols] + 0.05 * total * total
+            root = jnp.sqrt(second * (1.0 / (1.0 - 0.95**10))) + 1e-08
+            step = (first * (1.0 / (1.0 - 0.9**10))) / root
             out_ref[slot, 0, :, cols] = weight - 0.1 * (step + 0.3 * weight)
             out_ref[slot, 1, :, cols] = first
             out_ref[slot, 2, :, cols] = second
         return carry
 
-    lax.fori_loop(0, slots, update, 0, unroll=4)
+    lax.fori_loop(0, slots, update, 0, unroll=8)
 
 
 def shifted(value, axis, pairs_of):
@@ -62,22 +72,34 @@
     return total
 
 
+def plane_sum(value, slots, inner):
+    value = shifted(value, "expert", [[(i, i ^ 1) for i in range(slots)]])
+    return shifted(
+        value,
+        "expert",
+        [
+            [(i, i // inner * inner + (i + k) % inner) for i in range(slots)]
+            for k in range(2, inner, 2)
+        ],
+    )
+
+
 def all_sum(value):
     slots = lax.axis_size("expert")
     width = lax.axis_size("mp")
     inner = 8
-    outer = slots // inner
     value = shifted(
         value, "mp", [[(i, (i + k) % width) for i in range(width)] for k in range(1, width)]
     )
-    value = shifted(
-        value, "expert", [[(i, i ^ k) for i in range(slots)] for k in range(1, inner)]
-    )
-    return shifted(
-        value,
-        "expert",
-        [[(i, (i + k * inner) % slots) for i in range(slots)] for k in range(1, outer)],
-    )
+    value = plane_sum(value, slots, inner)
+    spots = [(i, (i + i % inner * inner) % slots) for i in range(slots) if i % inner]
+    moved = lax.ppermute(value, "expert", spots)
+    value = jnp.where(lax.axis_index("expert") % inner == 0, value, moved)
+    return plane_sum(value, slots, inner)
+
+
+def to_pieces(array):
+    return lax.all_to_all(array, "expert", split_axis=0, concat_axis=0, tiled=True)
 
 
 def on_device(
@@ -94,14 +116,17 @@
     lowest = jnp.argmax(equal, axis=1).astype(jnp.int32)
     source = jnp.where(place_now == place_next, jnp.arange(slots, dtype=jnp.int32), lowest)
 
+    weight_rows = weight.reshape(slots, rows, hidden)
+    first_rows = first_moment.reshape(slots, rows, hidden)
+    second_rows = second_moment.reshape(slots, rows, hidden)
+    weight_rows = to_pieces(weight_rows)
     grads = local_grad(tokens[0], cotangent[0], counts[0]).reshape(slots, rows, hidden)
-    states = jnp.stack(
-        [array.reshape(slots, rows, hidden) for array in (weight, first_moment, second_moment)],
-        axis=1,
-    )
-    spread = lax.all_to_all(grads, "expert", split_axis=0, concat_axis=0, tiled=True)
-    spread, states = lax.optimization_barrier((spread, states))
-    states = lax.all_to_all(states, "expert", split_axis=0, concat_axis=0, tiled=True)
+    weight_rows, grads = lax.optimization_barrier((weight_rows, grads))
+    spread = to_pieces(grads)
+    spread, first_rows = lax.optimization_barrier((spread, first_rows))
+    first_rows = to_pieces(first_rows)
+    first_rows, second_rows = lax.optimization_barrier((first_rows, second_rows))
+    second_rows = to_pieces(second_rows)
 
     smem = pl.BlockSpec(memory_space=pltpu.SMEM)
     part = pl.pallas_call(
@@ -125,12 +150,14 @@
             smem,
             pl.BlockSpec((8, LANES), lambda i: (0, 0)),
             pl.BlockSpec((slots, chunk, hidden), lambda i: (0, i, 0)),
-            pl.BlockSpec((slots, 3, chunk, hidden), lambda i: (0, 0, i, 0)),
+            pl.BlockSpec((slots, chunk, hidden), lambda i: (0, i, 0)),
+            pl.BlockSpec((slots, chunk, hidden), lambda i: (0, i, 0)),
+            pl.BlockSpec((slots, chunk, hidden), lambda i: (0, i, 0)),
         ],
         out_specs=pl.BlockSpec((slots, 3, chunk, hidden), lambda i: (0, 0, i, 0)),
         compiler_params=pltpu.CompilerParams(vmem_limit_bytes=32 * 2**20),
-    )(source, partner, sumsq, spread, states)
-    out = lax.all_to_all(out, "expert", split_axis=0, concat_axis=0, tiled=True)
+    )(source, partner, sumsq, spread, weight_rows, first_rows, second_rows)
+    out = to_pieces(out)
     return tuple(out[:, k].reshape(weight.shape) for k in range(3))
 
 

time: 301 us -> 321 us (1.066)
  blocking collectives: 117 us -> 204 us
  waiting for transfers between devices: 109 us -> 53.4 us
  starting transfers between devices: 49.2 us -> 42.5 us
  other arithmetic: 6.28 us -> 1.42 us
    all_to_all x1 -> x3, blocking collectives: 117 us -> 204 us  [to_pieces(): lax.all_to_all(array, 'expert', split_axis=0, concat_axis=0, tiled=True)]
    ppermute x17 -> x11, waiting for transfers between devices: 74.8 us -> 11.2 us  [shifted(): total = total + lax.ppermute(value, axis, pairs)]
    ppermute x0 -> x1, waiting for transfers between devices: none -> 10.2 us  [all_sum(): moved = lax.ppermute(value, 'expert', spots)]
    ppermute x17 -> x11, starting transfers between devices: 29.4 us -> 19.3 us  [shifted(): total = total + lax.ppermute(value, axis, pairs)]
    another operation x1 -> x0, other arithmetic: 4.86 us -> none  [on_device(): jnp.stack([array.reshape(slots, rows, hidden) for array in (weight, first...]
  transfers between devices with their start and end apart: 19 -> 14, of which waited for: 8 -> 10; matrix products, arithmetic and copies ran while one was open for 2% -> 2% of each run, Pallas kernels for 1% -> 1%
where the time goes in v2:
time: 321 us
  blocking collectives  204 us (64%)
  waiting for transfers between devices  53.4 us (17%)
  starting transfers between devices  42.5 us (13%)
  local copies, waits for them, and re-layouts  8.14 us (3%)
  Pallas kernels  6.39 us (2%)
  matrix products  3.28 us (1%)
    all_to_all x3, blocking collectives, to_pieces(): lax.all_to_all(array, 'expert', split_axis=0, concat_axis=0, tiled=True)  204 us
    all_to_all x2, waiting for transfers between devices, to_pieces(): lax.all_to_all(array, 'expert', split_axis=0, concat_axis=0, tiled=True)  32 us
    all_to_all x2, starting transfers between devices, to_pieces(): lax.all_to_all(array, 'expert', split_axis=0, concat_axis=0, tiled=True)  20.1 us
    ppermute x11, starting transfers between devices, shifted(): total = total + lax.ppermute(value, axis, pairs)  19.3 us
    ppermute x11, waiting for transfers between devices, shifted(): total = total + lax.ppermute(value, axis, pairs)  11.2 us
    ppermute x1, waiting for transfers between devices, all_sum(): moved = lax.ppermute(value, 'expert', spots)  10.2 us
  transfers between devices with their start and end apart: 14, of which 10 were waited for; matrix products, arithmetic and copies ran while one was open for 2% of the time, Pallas kernels for 1%

profile of v2, /device:TPU:1, one launch (start us, length us, event | category | flops | bytes accessed | tf_op | source)
XLA Modules:
  0.0 320.7 jit_solution(4562919141092177937)
XLA Ops:
  0.6 13.4 %all-to-all-start = ((f32[64,24,256]{2,1,0:T(8,128)}), f32[64,24,256]{2,1,0:T(8,128)}, u32[]{:S(2)}, u32[]{:S(2)}) async-start(f32[64,24,256]{2,1,0:T(8,128)} %bitcast.23), calls=%async_computation | async-start | bytes 3145728 | tf_op jit(solution)/shard_map/all_to_all | solution.py:102
  14.7 3.3 %fusion.2 = f32[1536,256]{0,1:T(8,128)} fusion(bf16[1,1024,1536]{2,1,0:T(8,128)(2,1)S(1)} %copy-done, bf16[1,1024,256]{2,1,0:T(8,128)(2,1)} %param.10, pred[1024]{0:T(1024)(128)(4,1)S(1)} %iota_compare_fusion), kind=kOutput, calls=%fused_computation.2 | convolution fusion | flops 805568512 | bytes 5243904 | tf_op jit(solution)/shard_map/rd,rh->dh/dot_general | solution.py:18
  18.0 3.0 copy.13
  21.1 32.0 %all-to-all-done.weight_ref = f32[64,24,256]{2,1,0:T(8,128)} async-done(((f32[64,24,256]{2,1,0:T(8,128)}), f32[64,24,256]{2,1,0:T(8,128)}, u32[]{:S(2)}, u32[]{:S(2)}) %all-to-all-start) | async-done | bytes 1572896 | tf_op jit(solution)/shard_map/all_to_all | solution.py:102
  53.0 45.7 %all_to_all.25.grad_ref = f32[64,24,256]{2,1,0:T(8,128)} all-to-all(f32[64,24,256]{2,1,0:T(8,128)} %bitcast.19), channel_id=1, replica_groups=mesh['expert'=64,'mp'=4] {'expert'}, dimensions={0} | all-to-all | bytes 3145728 | tf_op jit(solution)/shard_map/all_to_all | solution.py:102
  98.7 45.4 %all_to_all.26.first_ref = f32[64,24,256]{2,1,0:T(8,128)} all-to-all(f32[64,24,256]{2,1,0:T(8,128)S(1)} %bitcast.24), channel_id=1, replica_groups=mesh['expert'=64,'mp'=4] {'expert'}, dimensions={0} | all-to-all | bytes 3145728 | tf_op jit(solution)/shard_map/all_to_all | solution.py:102
  144.1 6.6 %all-to-all-start.3 = ((f32[64,24,256]{2,1,0:T(8,128)}), f32[64,24,256]{2,1,0:T(8,128)}, u32[]{:S(2)}, u32[]{:S(2)}) async-start(f32[64,24,256]{2,1,0:T(8,128)} %bitcast.25), calls=%async_computation.3 | async-start | bytes 3145728 | tf_op jit(solution)/shard_map/all_to_all | solution.py:102
  150.7 2.4 shard_map.112
  153.2 2.7 collective-permute-start.2
  155.9 0.3 collective-permute-start.1
  156.3 0.7 collective-permute-start
  157.0 3.5 %collective-permute-done.1 = f32[8,128]{1,0:T(8,128)S(1)} collective-permute-done((f32[8,128]{1,0:T(8,128)}, f32[8,128]{1,0:T(8,128)S(1)}, u32[]{:S(2)}, u32[]{:S(2)}) %collective-permute-start.1) | collective-permute-done | bytes 4128 | tf_op jit(solution)/shard_map/ppermute | solution.py:71
  160.5 0.7 add_add_fusion.2
  161.2 1.8 collective-permute-start.3
  163.1 0.8 collective-permute-done.3
  163.9 2.4 collective-permute-start.6
  166.3 0.6 collective-permute-start.5
  166.9 0.6 collective-permute-start.4
  167.5 3.2 %collective-permute-done.5 = f32[8,128]{1,0:T(8,128)S(1)} collective-permute-done((f32[8,128]{1,0:T(8,128)S(1)}, f32[8,128]{1,0:T(8,128)S(1)}, u32[]{:S(2)}, u32[]{:S(2)}) %collective-permute-start.5) | collective-permute-done | bytes 4128 | tf_op jit(solution)/shard_map/ppermute | solution.py:71
  171.1 3.2 collective-permute-start.7
  174.3 10.2 %collective-permute-done.7 = f32[8,128]{1,0:T(8,128)S(1)} collective-permute-done((f32[8,128]{1,0:T(8,128)S(1)}, f32[8,128]{1,0:T(8,128)S(1)}, u32[]{:S(2)}, u32[]{:S(2)}) %collective-permute-start.7) | collective-permute-done | bytes 4128 | tf_op jit(solution)/shard_map/ppermute | solution.py:96
  184.5 0.7 iota_reduce_fusion
  185.2 0.4 collective-permute-done.8
  185.6 4.0 %collective-permute-start.11 = (f32[8,128]{1,0:T(8,128)S(1)}, f32[8,128]{1,0:T(8,128)S(1)}, u32[]{:S(2)}, u32[]{:S(2)}) collective-permute-start(f32[8,128]{1,0:T(8,128)S(1)} %add.45), channel_id=1, source_target_pairs={{0,24},{4,28},{8,0},{12,4},{16,8},{20,12},{24,16},{28,20},{32,56},... | collective-permute-start | bytes 12296 | tf_op jit(solution)/shard_map/ppermute | solution.py:71
  189.6 5.3 %collective-permute-start.10 = (f32[8,128]{1,0:T(8,128)S(1)}, f32[8,128]{1,0:T(8,128)S(1)}, u32[]{:S(2)}, u32[]{:S(2)}) collective-permute-start(f32[8,128]{1,0:T(8,128)S(1)} %add.45), channel_id=1, source_target_pairs={{0,16},{4,20},{8,24},{12,28},{16,0},{20,4},{24,8},{28,12},{32,48},... | collective-permute-start | bytes 12296 | tf_op jit(solution)/shard_map/ppermute | solution.py:71
  194.8 0.9 collective-permute-start.9
  195.8 2.7 collective-permute-done.9
  198.5 1.4 copy-done.1
  199.9 1.4 copy-done.2
  201.3 4.0 %shard_map.113 = f32[64,3,24,256]{3,2,1,0:T(8,128)S(1)} custom-call(s32[64]{0:T(128)S(1)} %compare_select_fusion.source_ref, s32[64]{0:T(128)S(1)} %copy-done.3, f32[8,128]{1,0:T(8,128)S(1)} %add_add_fusion.sum_ref, f32[64,24,256]{2,1,0:T(8,128)S(1)} %copy-done.1, f32[64,24,256]{2,1,0:T(8,128)} %all-to-all-done.weight_ref, f32[64,24,256]{2,1,0:T(8,128)S(1)} %copy-done.2, ...), custom_call_target="tpu_custom_call" | custom-call | tf_op jit(solution)/shard_map/pallas_call | solution.py:144
  205.3 113.1 %all_to_all.27 = f32[64,3,24,256]{3,2,1,0:T(8,128)S(1)} all-to-all(f32[64,3,24,256]{3,2,1,0:T(8,128)S(1)} %shard_map.113), channel_id=1, replica_groups=mesh['expert'=64,'mp'=4] {'expert'}, dimensions={0} | all-to-all | bytes 9437184 | tf_op jit(solution)/shard_map/all_to_all | solution.py:102
  318.4 2.3 fusion.10
  (27 shorter events, 0.6 us)
Async XLA Ops:
  0.6 14.1 %copy-start = (bf16[1,1024,1536]{2,1,0:T(8,128)(2,1)S(1)}, bf16[1,1024,1536]{2,1,0:T(8,128)(2,1)}, u32[]{:S(2)}) copy-start(bf16[1,1024,1536]{2,1,0:T(8,128)(2,1)} %param.9) | copy-start | bytes 9437188
  0.6 52.4 %all-to-all-start = ((f32[64,24,256]{2,1,0:T(8,128)}), f32[64,24,256]{2,1,0:T(8,128)}, u32[]{:S(2)}, u32[]{:S(2)}) async-start(f32[64,24,256]{2,1,0:T(8,128)} %bitcast.23), calls=%async_computation | async-start | bytes 3145728 | tf_op jit(solution)/shard_map/all_to_all | solution.py:102
  53.0 45.7 %copy-start.4 = (f32[1,1536,256]{2,1,0:T(8,128)S(1)}, f32[1,1536,256]{2,1,0:T(8,128)}, u32[]{:S(2)}) copy-start(f32[1,1536,256]{2,1,0:T(8,128)} %param.16) | copy-start | bytes 4718596
  144.1 54.4 %all-to-all-start.3 = ((f32[64,24,256]{2,1,0:T(8,128)}), f32[64,24,256]{2,1,0:T(8,128)}, u32[]{:S(2)}, u32[]{:S(2)}) async-start(f32[64,24,256]{2,1,0:T(8,128)} %bitcast.25), calls=%async_computation.3 | async-start | bytes 3145728 | tf_op jit(solution)/shard_map/all_to_all | solution.py:102
  150.7 33.7 %copy-start.5 = (s32[64]{0:T(128)S(1)}, s32[64]{0:T(128)}, u32[]{:S(2)}) copy-start(s32[64]{0:T(128)} %param.12) | copy-start | bytes 772
  150.7 33.7 %copy-start.6 = (s32[64]{0:T(128)S(1)}, s32[64]{0:T(128)}, u32[]{:S(2)}) copy-start(s32[64]{0:T(128)} %param.14) | copy-start | bytes 772
  150.7 47.8 %copy-start.3 = (s32[64]{0:T(128)S(1)}, s32[64]{0:T(128)}, u32[]{:S(2)}) copy-start(s32[64]{0:T(128)} %partner_ref.3) | copy-start | bytes 772
  153.2 3.8 %collective-permute-start.2 = (f32[8,128]{1,0:T(8,128)}, f32[8,128]{1,0:T(8,128)S(1)}, u32[]{:S(2)}, u32[]{:S(2)}) collective-permute-start(f32[8,128]{1,0:T(8,128)} %shard_map.112), channel_id=1, source_target_pairs={{0,3},{1,0},{2,1},{3,2},{4,7},{5,4},{6,5},{7,6},{8,11},{9,8},{10,9... | collective-permute-start | bytes 12296 | tf_op jit(solution)/shard_map/ppermute | solution.py:71
  155.9 4.6 %collective-permute-start.1 = (f32[8,128]{1,0:T(8,128)}, f32[8,128]{1,0:T(8,128)S(1)}, u32[]{:S(2)}, u32[]{:S(2)}) collective-permute-start(f32[8,128]{1,0:T(8,128)} %shard_map.112), channel_id=1, source_target_pairs={{0,2},{1,3},{2,0},{3,1},{4,6},{5,7},{6,4},{7,5},{8,10},{9,11},{10,... | collective-permute-start | bytes 12296 | tf_op jit(solution)/shard_map/ppermute | solution.py:71
  156.3 4.3 %collective-permute-start = (f32[8,128]{1,0:T(8,128)}, f32[8,128]{1,0:T(8,128)S(1)}, u32[]{:S(2)}, u32[]{:S(2)}) collective-permute-start(f32[8,128]{1,0:T(8,128)} %shard_map.112), channel_id=1, source_target_pairs={{0,1},{1,2},{2,3},{3,0},{4,5},{5,6},{6,7},{7,4},{8,9},{9,10},{10,1... | collective-permute-start | bytes 12296 | tf_op jit(solution)/shard_map/ppermute | solution.py:71
  161.2 2.7 collective-permute-start.3
  163.9 3.6 %collective-permute-start.6 = (f32[8,128]{1,0:T(8,128)S(1)}, f32[8,128]{1,0:T(8,128)S(1)}, u32[]{:S(2)}, u32[]{:S(2)}) collective-permute-start(f32[8,128]{1,0:T(8,128)S(1)} %add.41), channel_id=1, source_target_pairs={{0,24},{4,28},{8,0},{12,4},{16,8},{20,12},{24,16},{28,20},{32,56},... | collective-permute-start | bytes 12296 | tf_op jit(solution)/shard_map/ppermute | solution.py:71
  166.3 4.4 %collective-permute-start.5 = (f32[8,128]{1,0:T(8,128)S(1)}, f32[8,128]{1,0:T(8,128)S(1)}, u32[]{:S(2)}, u32[]{:S(2)}) collective-permute-start(f32[8,128]{1,0:T(8,128)S(1)} %add.41), channel_id=1, source_target_pairs={{0,16},{4,20},{8,24},{12,28},{16,0},{20,4},{24,8},{28,12},{32,48},... | collective-permute-start | bytes 12296 | tf_op jit(solution)/shard_map/ppermute | solution.py:71
  166.9 4.1 %collective-permute-start.4 = (f32[8,128]{1,0:T(8,128)S(1)}, f32[8,128]{1,0:T(8,128)S(1)}, u32[]{:S(2)}, u32[]{:S(2)}) collective-permute-start(f32[8,128]{1,0:T(8,128)S(1)} %add.41), channel_id=1, source_target_pairs={{0,8},{4,12},{8,16},{12,20},{16,24},{20,28},{24,0},{28,4},{32,40},... | collective-permute-start | bytes 12296 | tf_op jit(solution)/shard_map/ppermute | solution.py:71
  171.1 13.4 %collective-permute-start.7 = (f32[8,128]{1,0:T(8,128)S(1)}, f32[8,128]{1,0:T(8,128)S(1)}, u32[]{:S(2)}, u32[]{:S(2)}) collective-permute-start(f32[8,128]{1,0:T(8,128)S(1)} %add_add_fusion.1), channel_id=1, source_target_pairs={{4,36},{8,72},{12,108},{16,144},{20,180},{24,216},{28,252},{36,68}... | collective-permute-start | bytes 12296 | tf_op jit(solution)/shard_map/ppermute | solution.py:96
  184.4 1.2 collective-permute-start.8
  185.6 10.1 %collective-permute-start.11 = (f32[8,128]{1,0:T(8,128)S(1)}, f32[8,128]{1,0:T(8,128)S(1)}, u32[]{:S(2)}, u32[]{:S(2)}) collective-permute-start(f32[8,128]{1,0:T(8,128)S(1)} %add.45), channel_id=1, source_target_pairs={{0,24},{4,28},{8,0},{12,4},{16,8},{20,12},{24,16},{28,20},{32,56},... | collective-permute-start | bytes 12296 | tf_op jit(solution)/shard_map/ppermute | solution.py:71
  189.6 6.3 %collective-permute-start.10 = (f32[8,128]{1,0:T(8,128)S(1)}, f32[8,128]{1,0:T(8,128)S(1)}, u32[]{:S(2)}, u32[]{:S(2)}) collective-permute-start(f32[8,128]{1,0:T(8,128)S(1)} %add.45), channel_id=1, source_target_pairs={{0,16},{4,20},{8,24},{12,28},{16,0},{20,4},{24,8},{28,12},{32,48},... | collective-permute-start | bytes 12296 | tf_op jit(solution)/shard_map/ppermute | solution.py:71
  194.8 3.7 %collective-permute-start.9 = (f32[8,128]{1,0:T(8,128)S(1)}, f32[8,128]{1,0:T(8,128)S(1)}, u32[]{:S(2)}, u32[]{:S(2)}) collective-permute-start(f32[8,128]{1,0:T(8,128)S(1)} %add.45), channel_id=1, source_target_pairs={{0,8},{4,12},{8,16},{12,20},{16,24},{20,28},{24,0},{28,4},{32,40},... | collective-permute-start | bytes 12296 | tf_op jit(solution)/shard_map/ppermute | solution.py:71
  198.5 1.4 copy-start.1
  199.9 1.4 copy-start.2

commit v3 on v2

v3 whole, which is shorter than its diff:
```python
import functools
import math

import jax
import jax.numpy as jnp
from jax import lax
from jax.experimental import pallas as pl
from jax.experimental.pallas import tpu as pltpu
from jax.sharding import PartitionSpec as P

LANES = 128
INNER = 8


def grad_kernel(live_ref, block_ref, rows_ref, out_ref):
    rows = rows_ref[...].astype(jnp.float32)
    row_ids = lax.broadcasted_iota(jnp.int32, rows.shape, 0)
    masked = jnp.where(row_ids < live_ref[0], rows, jnp.zeros_like(rows)).astype(jnp.bfloat16)
    out_ref[...] = lax.dot_general(
        block_ref[...], masked, (((0,), (0,)), ((), ())), preferred_element_type=jnp.float32
    )


def local_grad(block, grad_rows, live):
    rows, width = block.shape
    hidden = grad_rows.shape[1]
    tile = width // 2
    return pl.pallas_call(
        grad_kernel,
        grid=(width // tile,),
        out_shape=jax.ShapeDtypeStruct((width, hidden), jnp.float32),
        in_specs=[
            pl.BlockSpec(memory_space=pltpu.SMEM),
            pl.BlockSpec((rows, tile), lambda i: (0, i)),
            pl.BlockSpec((rows, hidden), lambda i: (0, 0)),
        ],
        out_specs=pl.BlockSpec((tile, hidden), lambda i: (i, 0)),
        compiler_params=pltpu.CompilerParams(vmem_limit_bytes=56 * 2**20),
        cost_estimate=pl.CostEstimate(
            flops=2 * rows * width * hidden,
            bytes_accessed=2 * rows * (width + hidden) + 4 * width * hidden,
            transcendentals=0,
        ),
    )(live, block, grad_rows)


def sumsq_kernel(slots, partner_ref, grad_ref, out_ref):
    def body(slot, acc):
        raw = grad_ref[slot] + grad_ref[partner_ref[slot]]
        return acc + raw * raw

    zero = jnp.zeros(grad_ref.shape[1:], jnp.float32)
    acc = lax.fori_loop(0, slots, body, zero, unroll=4)
    rows, cols = acc.shape
    part = sum(
        acc[r : r + 8, c : c + LANES] for r in range(0, rows, 8) for c in range(0, cols, LANES)
    )
    out_ref[...] = jnp.broadcast_to(0.5 * jnp.sum(part), out_ref.shape)


def update_kernel(
    slots,
    limit,
    source_ref,
    partner_ref,
    sum_ref,
    grad_ref,
    state_ref,
    out_ref,
):
    clip = jnp.minimum(jnp.float32(1.0), limit / jnp.sqrt(sum_ref[0:1, 0:1] + 1e-06))
    clip = jnp.broadcast_to(clip, (8, grad_ref.shape[2]))

    def update(slot, carry):
        source = source_ref[slot]
        other = partner_ref[source]
        for top in range(0, grad_ref.shape[1], 8):
            rows = pl.ds(top, 8)
            total = clip * (grad_ref[source, rows] + grad_ref[other, rows])
            weight = state_ref[source, 0, rows]
            first = 0.9 * state_ref[source, 1, rows] + 0.1 * total
            second = 0.95 * state_ref[source, 2, rows] + 0.05 * total * total
            root = jnp.sqrt(second * (1.0 / (1.0 - 0.95**10))) + 1e-08
            step = (first * (1.0 / (1.0 - 0.9**10))) / root
            out_ref[slot, 0, rows] = weight - 0.1 * (step + 0.3 * weight)
            out_ref[slot, 1, rows] = first
            out_ref[slot, 2, rows] = second
        return carry

    lax.fori_loop(0, slots, update, 0, unroll=4)


def shifted(value, axis, pairs_of):
    total = value
    for pairs in pairs_of:
        total = total + lax.ppermute(value, axis, pairs)
    return total


def plane_sum(value, slots, inner):
    value = shifted(value, "expert", [[(i, i ^ 1) for i in range(slots)]])
    return shifted(
        value,
        "expert",
        [
            [(i, i // inner * inner + (i + k) % inner) for i in range(slots)]
            for k in range(2, inner, 2)
        ],
    )


def all_sum(value):
    slots = lax.axis_size("expert")
    width = lax.axis_size("mp")
    value = shifted(
        value, "mp", [[(i, (i + k) % width) for i in range(width)] for k in range(1, width)]
    )
    value = plane_sum(value, slots, INNER)
    half = slots // INNER // 2
    core = lax.axis_index("expert") % 2
    total = jnp.where(core == 0, value, jnp.zeros_like(value))
    for k in range(half):
        spots = [
            (i, (i + (k + i % 2 * half) * INNER) % slots) for i in range(slots) if k + i % 2
        ]
        total = total + lax.ppermute(value, "expert", spots)
    return shifted(total, "expert", [[(i, i ^ 1) for i in range(slots)]])


def to_pieces(array):
    return lax.all_to_all(array, "expert", split_axis=0, concat_axis=0, tiled=True)


def on_device(
    tokens, cotangent, counts, place_now, partner, place_next, weight, first_moment, second_moment
):
    slots = lax.axis_size("expert")
    units = slots // 2
    width_dev = weight.shape[1]
    hidden = weight.shape[2]
    rows = width_dev // slots
    limit = 4.0 * math.sqrt(units * width_dev * lax.axis_size("mp") * hidden)

    pair = jnp.clip(partner, 0, slots - 1)
    equal = place_now[None, :] == place_next[:, None]
    lowest = jnp.argmax(equal, axis=1).astype(jnp.int32)
    source = jnp.where(place_now == place_next, jnp.arange(slots, dtype=jnp.int32), lowest)

    grads = local_grad(tokens[0], cotangent[0], counts).reshape(slots, rows, hidden)
    states = jnp.stack(
        [array.reshape(slots, rows, hidden) for array in (weight, first_moment, second_moment)],
        axis=1,
    )
    spread = to_pieces(grads)
    spread, states = lax.optimization_barrier((spread, states))
    states = to_pieces(states)

    smem = pl.BlockSpec(memory_space=pltpu.SMEM)
    part = pl.pallas_call(
        functools.partial(sumsq_kernel, slots),
        out_shape=jax.ShapeDtypeStruct((8, LANES), jnp.float32),
        in_specs=[smem, pl.BlockSpec(memory_space=pltpu.VMEM)],
        out_specs=pl.BlockSpec(memory_space=pltpu.VMEM),
        cost_estimate=pl.CostEstimate(
            flops=spread.size, bytes_accessed=spread.size * 4, transcendentals=0
        ),
    )(pair, spread)
    sumsq = all_sum(part)

    vmem = pl.BlockSpec(memory_space=pltpu.VMEM)
    out = pl.pallas_call(
        functools.partial(update_kernel, slots, limit),
        out_shape=jax.ShapeDtypeStruct((slots, 3, rows, hidden), jnp.float32),
        in_specs=[smem, smem, vmem, vmem, vmem],
        out_specs=vmem,
        compiler_params=pltpu.CompilerParams(vmem_limit_bytes=32 * 2**20),
    )(source, pair, sumsq, spread, states)
    out = to_pieces(out)
    return tuple(out[:, k].reshape(weight.shape) for k in range(3))


def solution(mesh):
    placed = (
        P("expert", None, "mp"),
        P("expert", None, None),
        P("expert"),
        P(),
        P(),
        P(),
        P("expert", "mp", None),
        P("expert", "mp", None),
        P("expert", "mp", None),
    )
    return jax.shard_map(
        on_device,
        mesh=mesh,
        in_specs=placed,
        out_specs=(P("expert", "mp", None), P("expert", "mp", None), P("expert", "mp", None)),
        check_vma=False,
    )
```

time: 321 us -> 293 us (0.913)
  blocking collectives: 204 us -> 115 us
  waiting for transfers between devices: 53.4 us -> 113 us
  other arithmetic: 1.42 us -> 6.51 us
  local copies, waits for them, and re-layouts: 8.14 us -> 3.45 us
  Pallas kernels: 6.39 us -> 10.1 us
  matrix products: 3.28 us -> 0 us
    all_to_all x3 -> x1, blocking collectives: 204 us -> 115 us  [to_pieces(): lax.all_to_all(array, 'expert', split_axis=0, concat_axis=0, tiled=True)]
    ppermute x1 -> x4, waiting for transfers between devices: 10.2 us -> 73.6 us  [all_sum(): total = total + lax.ppermute(value, 'expert', spots)]
    ppermute x1 -> x4, starting transfers between devices: 3.17 us -> 11.2 us  [all_sum(): total = total + lax.ppermute(value, 'expert', spots)]
    ppermute x11 -> x8, starting transfers between devices: 19.3 us -> 12.5 us  [shifted(): total = total + lax.ppermute(value, axis, pairs)]
    ppermute x11 -> x8, waiting for transfers between devices: 11.2 us -> 5.33 us  [shifted(): total = total + lax.ppermute(value, axis, pairs)]
    another operation x0 -> x1, other arithmetic: none -> 4.58 us  [on_device(): jnp.stack([array.reshape(slots, rows, hidden) for array in (weight, first...]
    pallas_call x1 -> x2, Pallas kernels: 3.96 us -> 7.69 us  [the longest x1 4.02 us: on_device(): pl.pallas_call(functools.partial(update_kernel, slots, limit), out_shape=...]
    dot_general x1 -> x0, matrix products: 3.28 us -> none  [local_grad(): jnp.einsum('rd,rh->dh', block, masked, preferred_element_type=jnp.float32)]
  transfers between devices with their start and end apart: 14 -> 14, of which waited for: 10 -> 9; matrix products, arithmetic and copies ran while one was open for 2% -> 2% of each run, Pallas kernels for 1% -> 1%
where the time goes in v3:
time: 293 us
  blocking collectives  115 us (39%)
  waiting for transfers between devices  113 us (39%)
  starting transfers between devices  43.5 us (15%)
  Pallas kernels  10.1 us (3%)
  other arithmetic  6.51 us (2%)
  local copies, waits for them, and re-layouts  3.45 us (1%)
    all_to_all x1, blocking collectives, to_pieces(): lax.all_to_all(array, 'expert', split_axis=0, concat_axis=0, tiled=True)  115 us
    ppermute x4, waiting for transfers between devices, all_sum(): total = total + lax.ppermute(value, 'expert', spots)  73.6 us
    all_to_all x2, waiting for transfers between devices, to_pieces(): lax.all_to_all(array, 'expert', split_axis=0, concat_axis=0, tiled=True)  34.4 us
    all_to_all x2, starting transfers between devices, to_pieces(): lax.all_to_all(array, 'expert', split_axis=0, concat_axis=0, tiled=True)  19.7 us
    ppermute x8, starting transfers between devices, shifted(): total = total + lax.ppermute(value, axis, pairs)  12.5 us
    ppermute x4, starting transfers between devices, all_sum(): total = total + lax.ppermute(value, 'expert', spots)  11.2 us
  transfers between devices with their start and end apart: 14, of which 9 were waited for; matrix products, arithmetic and copies ran while one was open for 2% of the time, Pallas kernels for 1%

profile of v3, /device:TPU:1, one launch (start us, length us, event | category | flops | bytes accessed | tf_op | source)
XLA Modules:
  0.0 293.0 jit_solution(10875039040532248855)
XLA Ops:
  1.3 3.7 %shard_map.112 = f32[1536,256]{1,0:T(8,128)} custom-call(s32[1]{0:T(128)S(6)} %copy.12.live_ref, bf16[1024,1536]{1,0:T(8,128)(2,1)} %bitcast.10, bf16[1024,256]{1,0:T(8,128)(2,1)} %bitcast.17), custom_call_target="tpu_custom_call" | custom-call | flops 805306368 | bytes 5242880 | tf_op jit(solution)/shard_map/pallas_call | solution.py:28
  4.9 13.1 %all-to-all-start = ((f32[64,24,256]{2,1,0:T(8,128)}), f32[64,24,256]{2,1,0:T(8,128)S(1)}, u32[]{:S(2)}, u32[]{:S(2)}) async-start(f32[64,24,256]{2,1,0:T(8,128)} %bitcast.9), calls=%async_computation | async-start | bytes 3145728 | tf_op jit(solution)/shard_map/all_to_all | solution.py:131
  18.1 4.6 %pad_maximum_fusion = f32[64,3,24,256]{3,2,1,0:T(8,128)} fusion(f32[64,1,24,256]{3,2,1,0:T(8,128)S(1)} %bitcast.11, f32[64,1,24,256]{3,2,1,0:T(8,128)} %bitcast.12, f32[64,1,24,256]{3,2,1,0:T(8,128)} %bitcast.13), kind=kLoop, calls=%fused_computation | loop fusion | flops 2359296 | bytes 9437184 | tf_op jit(solution)/shard_map/stack | solution.py:150
  22.7 34.4 %all-to-all-done.grad_ref = f32[64,24,256]{2,1,0:T(8,128)S(1)} async-done(((f32[64,24,256]{2,1,0:T(8,128)}), f32[64,24,256]{2,1,0:T(8,128)S(1)}, u32[]{:S(2)}, u32[]{:S(2)}) %all-to-all-start) | async-done | bytes 1572896 | tf_op jit(solution)/shard_map/all_to_all | solution.py:131
  57.1 1.1 copy-done
  58.2 6.6 %all-to-all-start.1 = ((f32[64,3,24,256]{3,2,1,0:T(8,128)}), f32[64,3,24,256]{3,2,1,0:T(8,128)}, u32[]{:S(2)}, u32[]{:S(2)}) async-start(f32[64,3,24,256]{3,2,1,0:T(8,128)} %pad_maximum_fusion), calls=%async_computation.1 | async-start | bytes 9437184 | tf_op jit(solution)/shard_map/all_to_all | solution.py:131
  64.9 0.5 broadcast_clamp_fusion.partner_ref
  65.4 2.4 shard_map.113
  67.8 1.3 collective-permute-start
  69.1 2.6 collective-permute-start.1
  71.8 1.1 collective-permute-start.2
  72.8 0.9 collective-permute-done.1
  73.7 1.1 collective-permute-done.2
  74.8 0.7 add_add_fusion.2
  75.5 1.9 collective-permute-start.3
  77.5 0.8 collective-permute-done.3
  78.3 1.1 collective-permute-start.4
  79.4 2.4 collective-permute-start.5
  81.8 1.2 collective-permute-start.6
  83.0 0.8 collective-permute-done.5
  83.8 0.9 collective-permute-done.6
  84.7 2.8 collective-permute-start.10
  87.5 4.7 %collective-permute-start.7 = (f32[8,128]{1,0:T(8,128)S(1)}, f32[8,128]{1,0:T(8,128)S(1)}, u32[]{:S(2)}, u32[]{:S(2)}) collective-permute-start(f32[8,128]{1,0:T(8,128)S(1)} %add_add_fusion.1), channel_id=1, source_target_pairs={{4,132},{12,140},{20,148},{28,156},{36,164},{44,172},{52,180},{60,... | collective-permute-start | bytes 12296 | tf_op jit(solution)/shard_map/ppermute | solution.py:126
  92.3 3.6 %collective-permute-start.9 = (f32[8,128]{1,0:T(8,128)S(1)}, f32[8,128]{1,0:T(8,128)S(1)}, u32[]{:S(2)}, u32[]{:S(2)}) collective-permute-start(f32[8,128]{1,0:T(8,128)S(1)} %add_add_fusion.1), channel_id=1, source_target_pairs={{0,64},{4,196},{8,72},{12,204},{16,80},{20,212},{24,88},{28,220},{... | collective-permute-start | bytes 12296 | tf_op jit(solution)/shard_map/ppermute | solution.py:126
  96.0 0.7 iota_reduce_fusion
  96.7 70.2 %collective-permute-done.10 = f32[8,128]{1,0:T(8,128)S(1)} collective-permute-done((f32[8,128]{1,0:T(8,128)S(1)}, f32[8,128]{1,0:T(8,128)S(1)}, u32[]{:S(2)}, u32[]{:S(2)}) %collective-permute-start.10) | collective-permute-done | bytes 4128 | tf_op jit(solution)/shard_map/ppermute | solution.py:126
  166.9 3.4 %collective-permute-done.7 = f32[8,128]{1,0:T(8,128)S(1)} collective-permute-done((f32[8,128]{1,0:T(8,128)S(1)}, f32[8,128]{1,0:T(8,128)S(1)}, u32[]{:S(2)}, u32[]{:S(2)}) %collective-permute-start.7) | collective-permute-done | bytes 4128 | tf_op jit(solution)/shard_map/ppermute | solution.py:126
  170.3 0.8 collective-permute-start.11
  171.1 0.8 collective-permute-done.11
  172.0 4.0 %shard_map.114 = f32[64,3,24,256]{3,2,1,0:T(8,128)S(1)} custom-call(s32[64]{0:T(128)S(1)} %compare_select_fusion.source_ref, s32[64]{0:T(128)S(1)} %copy-done.2, f32[8,128]{1,0:T(8,128)S(1)} %add.52.sum_ref, f32[64,24,256]{2,1,0:T(8,128)S(1)} %copy-done.1, f32[64,3,24,256]{3,2,1,0:T(8,128)} %all-to-all-done.1.state_ref), custom_call_target="tpu_custom_call" | custom-call | tf_op jit(solution)/shard_map/pallas_call | solution.py:171
  176.0 114.7 %all_to_all.15 = f32[64,3,24,256]{3,2,1,0:T(8,128)S(1)} all-to-all(f32[64,3,24,256]{3,2,1,0:T(8,128)S(1)} %shard_map.114), channel_id=1, replica_groups=mesh['expert'=64,'mp'=4] {'expert'}, dimensions={0} | all-to-all | bytes 9437184 | tf_op jit(solution)/shard_map/all_to_all | solution.py:131
  290.7 2.3 fusion
  (24 shorter events, 0.3 us)
Async XLA Ops:
  4.9 13.1 %copy-start.3 = (f32[1,1536,256]{2,1,0:T(8,128)S(1)}, f32[1,1536,256]{2,1,0:T(8,128)}, u32[]{:S(2)}) copy-start(f32[1,1536,256]{2,1,0:T(8,128)} %param.17) | copy-start | bytes 4718596
  4.9 52.1 %all-to-all-start = ((f32[64,24,256]{2,1,0:T(8,128)}), f32[64,24,256]{2,1,0:T(8,128)S(1)}, u32[]{:S(2)}, u32[]{:S(2)}) async-start(f32[64,24,256]{2,1,0:T(8,128)} %bitcast.9), calls=%async_computation | async-start | bytes 3145728 | tf_op jit(solution)/shard_map/all_to_all | solution.py:131
  22.7 42.2 %copy-start.6 = (s32[64]{0:T(128)S(1)}, s32[64]{0:T(128)}, u32[]{:S(2)}) copy-start(s32[64]{0:T(128)} %param.13) | copy-start | bytes 772
  57.1 1.1 copy-start
  58.2 113.8 %all-to-all-start.1 = ((f32[64,3,24,256]{3,2,1,0:T(8,128)}), f32[64,3,24,256]{3,2,1,0:T(8,128)}, u32[]{:S(2)}, u32[]{:S(2)}) async-start(f32[64,3,24,256]{3,2,1,0:T(8,128)} %pad_maximum_fusion), calls=%async_computation.1 | async-start | bytes 9437184 | tf_op jit(solution)/shard_map/all_to_all | solution.py:131
  64.9 31.1 %copy-start.4 = (s32[64]{0:T(128)S(1)}, s32[64]{0:T(128)}, u32[]{:S(2)}) copy-start(s32[64]{0:T(128)} %param.12) | copy-start | bytes 772
  64.9 31.1 %copy-start.5 = (s32[64]{0:T(128)S(1)}, s32[64]{0:T(128)}, u32[]{:S(2)}) copy-start(s32[64]{0:T(128)} %param.14) | copy-start | bytes 772
  64.9 107.1 %copy-start.1 = (f32[64,24,256]{2,1,0:T(8,128)S(1)}, f32[64,24,256]{2,1,0:T(8,128)}, u32[]{:S(2)}) copy-start(f32[64,24,256]{2,1,0:T(8,128)} %copy-done) | copy-start | bytes 4718596
  65.4 106.6 %copy-start.2 = (s32[64]{0:T(128)S(1)}, s32[64]{0:T(128)}, u32[]{:S(2)}) copy-start(s32[64]{0:T(128)} %broadcast_clamp_fusion.partner_ref) | copy-start | bytes 772
  67.8 5.0 %collective-permute-start = (f32[8,128]{1,0:T(8,128)}, f32[8,128]{1,0:T(8,128)S(1)}, u32[]{:S(2)}, u32[]{:S(2)}) collective-permute-start(f32[8,128]{1,0:T(8,128)} %shard_map.113), channel_id=1, source_target_pairs={{0,1},{1,2},{2,3},{3,0},{4,5},{5,6},{6,7},{7,4},{8,9},{9,10},{10,1... | collective-permute-start | bytes 12296 | tf_op jit(solution)/shard_map/ppermute | solution.py:96
  69.1 4.6 %collective-permute-start.1 = (f32[8,128]{1,0:T(8,128)}, f32[8,128]{1,0:T(8,128)S(1)}, u32[]{:S(2)}, u32[]{:S(2)}) collective-permute-start(f32[8,128]{1,0:T(8,128)} %shard_map.113), channel_id=1, source_target_pairs={{0,2},{1,3},{2,0},{3,1},{4,6},{5,7},{6,4},{7,5},{8,10},{9,11},{10,... | collective-permute-start | bytes 12296 | tf_op jit(solution)/shard_map/ppermute | solution.py:96
  71.8 3.1 %collective-permute-start.2 = (f32[8,128]{1,0:T(8,128)}, f32[8,128]{1,0:T(8,128)S(1)}, u32[]{:S(2)}, u32[]{:S(2)}) collective-permute-start(f32[8,128]{1,0:T(8,128)} %shard_map.113), channel_id=1, source_target_pairs={{0,3},{1,0},{2,1},{3,2},{4,7},{5,4},{6,5},{7,6},{8,11},{9,8},{10,9... | collective-permute-start | bytes 12296 | tf_op jit(solution)/shard_map/ppermute | solution.py:96
  75.5 2.8 collective-permute-start.3
  78.3 4.7 %collective-permute-start.4 = (f32[8,128]{1,0:T(8,128)S(1)}, f32[8,128]{1,0:T(8,128)S(1)}, u32[]{:S(2)}, u32[]{:S(2)}) collective-permute-start(f32[8,128]{1,0:T(8,128)S(1)} %add.44), channel_id=1, source_target_pairs={{0,8},{4,12},{8,16},{12,20},{16,24},{20,28},{24,0},{28,4},{32,40},... | collective-permute-start | bytes 12296 | tf_op jit(solution)/shard_map/ppermute | solution.py:96
  79.4 4.4 %collective-permute-start.5 = (f32[8,128]{1,0:T(8,128)S(1)}, f32[8,128]{1,0:T(8,128)S(1)}, u32[]{:S(2)}, u32[]{:S(2)}) collective-permute-start(f32[8,128]{1,0:T(8,128)S(1)} %add.44), channel_id=1, source_target_pairs={{0,16},{4,20},{8,24},{12,28},{16,0},{20,4},{24,8},{28,12},{32,48},... | collective-permute-start | bytes 12296 | tf_op jit(solution)/shard_map/ppermute | solution.py:96
  81.8 2.9 collective-permute-start.6
  84.7 82.2 %collective-permute-start.10 = (f32[8,128]{1,0:T(8,128)S(1)}, f32[8,128]{1,0:T(8,128)S(1)}, u32[]{:S(2)}, u32[]{:S(2)}) collective-permute-start(f32[8,128]{1,0:T(8,128)S(1)} %add_add_fusion.1), channel_id=1, source_target_pairs={{0,96},{4,228},{8,104},{12,236},{16,112},{20,244},{24,120},{28,252... | collective-permute-start | bytes 12296 | tf_op jit(solution)/shard_map/ppermute | solution.py:126
  87.5 82.8 %collective-permute-start.7 = (f32[8,128]{1,0:T(8,128)S(1)}, f32[8,128]{1,0:T(8,128)S(1)}, u32[]{:S(2)}, u32[]{:S(2)}) collective-permute-start(f32[8,128]{1,0:T(8,128)S(1)} %add_add_fusion.1), channel_id=1, source_target_pairs={{4,132},{12,140},{20,148},{28,156},{36,164},{44,172},{52,180},{60,... | collective-permute-start | bytes 12296 | tf_op jit(solution)/shard_map/ppermute | solution.py:126
  92.1 78.1 %collective-permute-start.8 = (f32[8,128]{1,0:T(8,128)S(1)}, f32[8,128]{1,0:T(8,128)S(1)}, u32[]{:S(2)}, u32[]{:S(2)}) collective-permute-start(f32[8,128]{1,0:T(8,128)S(1)} %add_add_fusion.1), channel_id=1, source_target_pairs={{0,32},{4,164},{8,40},{12,172},{16,48},{20,180},{24,56},{28,188},{... | collective-permute-start | bytes 12296 | tf_op jit(solution)/shard_map/ppermute | solution.py:126
  92.3 78.0 %collective-permute-start.9 = (f32[8,128]{1,0:T(8,128)S(1)}, f32[8,128]{1,0:T(8,128)S(1)}, u32[]{:S(2)}, u32[]{:S(2)}) collective-permute-start(f32[8,128]{1,0:T(8,128)S(1)} %add_add_fusion.1), channel_id=1, source_target_pairs={{0,64},{4,196},{8,72},{12,204},{16,80},{20,212},{24,88},{28,220},{... | collective-permute-start | bytes 12296 | tf_op jit(solution)/shard_map/ppermute | solution.py:126
  170.3 1.7 collective-permute-start.11

commit v4 on v3

--- a/solution.py
+++ b/solution.py
@@ -161,6 +161,7 @@
         out_shape=jax.ShapeDtypeStruct((8, LANES), jnp.float32),
         in_specs=[smem, pl.BlockSpec(memory_space=pltpu.VMEM)],
         out_specs=pl.BlockSpec(memory_space=pltpu.VMEM),
+        compiler_params=pltpu.CompilerParams(vmem_limit_bytes=8 * 2**20),
         cost_estimate=pl.CostEstimate(
             flops=spread.size, bytes_accessed=spread.size * 4, transcendentals=0
         ),
@@ -173,7 +174,7 @@
         out_shape=jax.ShapeDtypeStruct((slots, 3, rows, hidden), jnp.float32),
         in_specs=[smem, smem, vmem, vmem, vmem],
         out_specs=vmem,
-        compiler_params=pltpu.CompilerParams(vmem_limit_bytes=32 * 2**20),
+        compiler_params=pltpu.CompilerParams(vmem_limit_bytes=16 * 2**20),
     )(source, pair, sumsq, spread, states)
     out = to_pieces(out)
     return tuple(out[:, k].reshape(weight.shape) for k in range(3))

time: 293 us -> 292 us (level)
  transfers between devices with their start and end apart: 14 -> 14, of which waited for: 9 -> 9; matrix products, arithmetic and copies ran while one was open for 2% -> 2% of each run, Pallas kernels for 1% -> 0%
where the time goes in v4:
time: 292 us
  waiting for transfers between devices  115 us (39%)
  blocking collectives  115 us (39%)
  starting transfers between devices  44.1 us (15%)
  Pallas kernels  8.62 us (3%)
  other arithmetic  5.31 us (2%)
    all_to_all x1, blocking collectives, to_pieces(): lax.all_to_all(array, 'expert', split_axis=0, concat_axis=0, tiled=True)  115 us
    ppermute x4, waiting for transfers between devices, all_sum(): total = total + lax.ppermute(value, 'expert', spots)  75.9 us
    all_to_all x2, waiting for transfers between devices, to_pieces(): lax.all_to_all(array, 'expert', split_axis=0, concat_axis=0, tiled=True)  34.4 us
    all_to_all x2, starting transfers between devices, to_pieces(): lax.all_to_all(array, 'expert', split_axis=0, concat_axis=0, tiled=True)  19.7 us
    ppermute x8, starting transfers between devices, shifted(): total = total + lax.ppermute(value, axis, pairs)  12.6 us
    ppermute x4, starting transfers between devices, all_sum(): total = total + lax.ppermute(value, 'expert', spots)  11.7 us
  transfers between devices with their start and end apart: 14, of which 9 were waited for; matrix products, arithmetic and copies ran while one was open for 2% of the time, Pallas kernels for 0%

profile of v4, /device:TPU:1, one launch (start us, length us, event | category | flops | bytes accessed | tf_op | source)
XLA Modules:
  0.0 291.8 jit_solution(11208567684957873169)
XLA Ops:
  1.3 3.7 %shard_map.112 = f32[1536,256]{1,0:T(8,128)} custom-call(s32[1]{0:T(128)S(6)} %copy.12.live_ref, bf16[1024,1536]{1,0:T(8,128)(2,1)} %bitcast.10, bf16[1024,256]{1,0:T(8,128)(2,1)} %bitcast.17), custom_call_target="tpu_custom_call" | custom-call | flops 805306368 | bytes 5242880 | tf_op jit(solution)/shard_map/pallas_call | solution.py:28
  4.9 13.1 %all-to-all-start = ((f32[64,24,256]{2,1,0:T(8,128)}), f32[64,24,256]{2,1,0:T(8,128)S(1)}, u32[]{:S(2)}, u32[]{:S(2)}) async-start(f32[64,24,256]{2,1,0:T(8,128)} %bitcast.9), calls=%async_computation | async-start | bytes 3145728 | tf_op jit(solution)/shard_map/all_to_all | solution.py:131
  18.1 4.6 %pad_maximum_fusion = f32[64,3,24,256]{3,2,1,0:T(8,128)} fusion(f32[64,1,24,256]{3,2,1,0:T(8,128)S(1)} %bitcast.11, f32[64,1,24,256]{3,2,1,0:T(8,128)} %bitcast.12, f32[64,1,24,256]{3,2,1,0:T(8,128)} %bitcast.13), kind=kLoop, calls=%fused_computation | loop fusion | flops 2359296 | bytes 9437184 | tf_op jit(solution)/shard_map/stack | solution.py:150
  22.7 34.4 %all-to-all-done.grad_ref = f32[64,24,256]{2,1,0:T(8,128)S(1)} async-done(((f32[64,24,256]{2,1,0:T(8,128)}), f32[64,24,256]{2,1,0:T(8,128)S(1)}, u32[]{:S(2)}, u32[]{:S(2)}) %all-to-all-start) | async-done | bytes 1572896 | tf_op jit(solution)/shard_map/all_to_all | solution.py:131
  57.1 6.6 %all-to-all-start.1 = ((f32[64,3,24,256]{3,2,1,0:T(8,128)}), f32[64,3,24,256]{3,2,1,0:T(8,128)}, u32[]{:S(2)}, u32[]{:S(2)}) async-start(f32[64,3,24,256]{3,2,1,0:T(8,128)} %pad_maximum_fusion), calls=%async_computation.1 | async-start | bytes 9437184 | tf_op jit(solution)/shard_map/all_to_all | solution.py:131
  63.7 0.0 copy-start.1
  63.7 0.0 copy-start.2
  63.8 0.9 shard_map.113
  64.7 1.4 collective-permute-start
  66.1 2.6 collective-permute-start.1
  68.7 1.1 collective-permute-start.2
  69.8 0.5 collective-permute-done.1
  70.3 1.3 collective-permute-done.2
  71.6 1.9 collective-permute-start.3
  73.5 0.8 collective-permute-done.3
  74.3 1.1 collective-permute-start.4
  75.4 2.4 collective-permute-start.5
  77.9 1.2 collective-permute-start.6
  79.0 0.8 collective-permute-done.5
  79.8 0.9 collective-permute-done.6
  80.8 2.8 collective-permute-start.10
  83.5 5.4 %collective-permute-start.7 = (f32[8,128]{1,0:T(8,128)S(1)}, f32[8,128]{1,0:T(8,128)S(1)}, u32[]{:S(2)}, u32[]{:S(2)}) collective-permute-start(f32[8,128]{1,0:T(8,128)S(1)} %add_add_fusion.1), channel_id=1, source_target_pairs={{4,132},{12,140},{20,148},{28,156},{36,164},{44,172},{52,180},{60,... | collective-permute-start | bytes 12296 | tf_op jit(solution)/shard_map/ppermute | solution.py:126
  88.9 0.3 collective-permute-start.8
  89.2 3.3 %collective-permute-start.9 = (f32[8,128]{1,0:T(8,128)S(1)}, f32[8,128]{1,0:T(8,128)S(1)}, u32[]{:S(2)}, u32[]{:S(2)}) collective-permute-start(f32[8,128]{1,0:T(8,128)S(1)} %add_add_fusion.1), channel_id=1, source_target_pairs={{0,64},{4,196},{8,72},{12,204},{16,80},{20,212},{24,88},{28,220},{... | collective-permute-start | bytes 12296 | tf_op jit(solution)/shard_map/ppermute | solution.py:126
  92.5 0.7 iota_reduce_fusion
  93.2 72.5 %collective-permute-done.10 = f32[8,128]{1,0:T(8,128)S(1)} collective-permute-done((f32[8,128]{1,0:T(8,128)S(1)}, f32[8,128]{1,0:T(8,128)S(1)}, u32[]{:S(2)}, u32[]{:S(2)}) %collective-permute-start.10) | collective-permute-done | bytes 4128 | tf_op jit(solution)/shard_map/ppermute | solution.py:126
  165.7 3.4 %collective-permute-done.7 = f32[8,128]{1,0:T(8,128)S(1)} collective-permute-done((f32[8,128]{1,0:T(8,128)S(1)}, f32[8,128]{1,0:T(8,128)S(1)}, u32[]{:S(2)}, u32[]{:S(2)}) %collective-permute-start.7) | collective-permute-done | bytes 4128 | tf_op jit(solution)/shard_map/ppermute | solution.py:126
  169.1 0.9 collective-permute-start.11
  170.0 0.8 collective-permute-done.11
  170.8 4.0 %shard_map.114 = f32[64,3,24,256]{3,2,1,0:T(8,128)S(1)} custom-call(s32[64]{0:T(128)S(1)} %compare_select_fusion.source_ref, s32[64]{0:T(128)S(1)} %broadcast_clamp_fusion.partner_ref, f32[8,128]{1,0:T(8,128)S(1)} %add.52.sum_ref, f32[64,24,256]{2,1,0:T(8,128)S(1)} %all-to-all-done.grad_ref, f32[64,3,24,256]{3,2,1,0:T(8,128)} %all-to-all-done.1.state_ref), custom_call_target="tpu_custom_call" | custom-call | tf_op jit(solution)/shard_map/pallas_call | solution.py:172
  174.9 114.7 %all_to_all.15 = f32[64,3,24,256]{3,2,1,0:T(8,128)S(1)} all-to-all(f32[64,3,24,256]{3,2,1,0:T(8,128)S(1)} %shard_map.114), channel_id=1, replica_groups=mesh['expert'=64,'mp'=4] {'expert'}, dimensions={0} | all-to-all | bytes 9437184 | tf_op jit(solution)/shard_map/all_to_all | solution.py:131
  289.5 2.3 fusion
  (18 shorter events, 0.1 us)
Async XLA Ops:
  4.9 13.1 %copy-start = (f32[1,1536,256]{2,1,0:T(8,128)S(1)}, f32[1,1536,256]{2,1,0:T(8,128)}, u32[]{:S(2)}) copy-start(f32[1,1536,256]{2,1,0:T(8,128)} %param.17) | copy-start | bytes 4718596
  4.9 52.1 %all-to-all-start = ((f32[64,24,256]{2,1,0:T(8,128)}), f32[64,24,256]{2,1,0:T(8,128)S(1)}, u32[]{:S(2)}, u32[]{:S(2)}) async-start(f32[64,24,256]{2,1,0:T(8,128)} %bitcast.9), calls=%async_computation | async-start | bytes 3145728 | tf_op jit(solution)/shard_map/all_to_all | solution.py:131
  22.7 41.0 %copy-start.3 = (s32[64]{0:T(128)S(1)}, s32[64]{0:T(128)}, u32[]{:S(2)}) copy-start(s32[64]{0:T(128)} %param.13) | copy-start | bytes 772
  57.1 113.8 %all-to-all-start.1 = ((f32[64,3,24,256]{3,2,1,0:T(8,128)}), f32[64,3,24,256]{3,2,1,0:T(8,128)}, u32[]{:S(2)}, u32[]{:S(2)}) async-start(f32[64,3,24,256]{3,2,1,0:T(8,128)} %pad_maximum_fusion), calls=%async_computation.1 | async-start | bytes 9437184 | tf_op jit(solution)/shard_map/all_to_all | solution.py:131
  63.7 28.8 %copy-start.1 = (s32[64]{0:T(128)S(1)}, s32[64]{0:T(128)}, u32[]{:S(2)}) copy-start(s32[64]{0:T(128)} %param.12) | copy-start | bytes 772
  63.7 28.8 %copy-start.2 = (s32[64]{0:T(128)S(1)}, s32[64]{0:T(128)}, u32[]{:S(2)}) copy-start(s32[64]{0:T(128)} %param.14) | copy-start | bytes 772
  64.7 5.1 %collective-permute-start = (f32[8,128]{1,0:T(8,128)S(1)}, f32[8,128]{1,0:T(8,128)S(1)}, u32[]{:S(2)}, u32[]{:S(2)}) collective-permute-start(f32[8,128]{1,0:T(8,128)S(1)} %shard_map.113), channel_id=1, source_target_pairs={{0,1},{1,2},{2,3},{3,0},{4,5},{5,6},{6,7},{7,4},{8,9},{9,10},{10,1... | collective-permute-start | bytes 12296 | tf_op jit(solution)/shard_map/ppermute | solution.py:96
  66.1 4.2 %collective-permute-start.1 = (f32[8,128]{1,0:T(8,128)S(1)}, f32[8,128]{1,0:T(8,128)S(1)}, u32[]{:S(2)}, u32[]{:S(2)}) collective-permute-start(f32[8,128]{1,0:T(8,128)S(1)} %shard_map.113), channel_id=1, source_target_pairs={{0,2},{1,3},{2,0},{3,1},{4,6},{5,7},{6,4},{7,5},{8,10},{9,11},{10,... | collective-permute-start | bytes 12296 | tf_op jit(solution)/shard_map/ppermute | solution.py:96
  68.7 2.9 collective-permute-start.2
  71.6 2.8 collective-permute-start.3
  74.3 4.7 %collective-permute-start.4 = (f32[8,128]{1,0:T(8,128)S(1)}, f32[8,128]{1,0:T(8,128)S(1)}, u32[]{:S(2)}, u32[]{:S(2)}) collective-permute-start(f32[8,128]{1,0:T(8,128)S(1)} %add.44), channel_id=1, source_target_pairs={{0,8},{4,12},{8,16},{12,20},{16,24},{20,28},{24,0},{28,4},{32,40},... | collective-permute-start | bytes 12296 | tf_op jit(solution)/shard_map/ppermute | solution.py:96
  75.4 4.4 %collective-permute-start.5 = (f32[8,128]{1,0:T(8,128)S(1)}, f32[8,128]{1,0:T(8,128)S(1)}, u32[]{:S(2)}, u32[]{:S(2)}) collective-permute-start(f32[8,128]{1,0:T(8,128)S(1)} %add.44), channel_id=1, source_target_pairs={{0,16},{4,20},{8,24},{12,28},{16,0},{20,4},{24,8},{28,12},{32,48},... | collective-permute-start | bytes 12296 | tf_op jit(solution)/shard_map/ppermute | solution.py:96
  77.9 2.9 collective-permute-start.6
  80.8 85.0 %collective-permute-start.10 = (f32[8,128]{1,0:T(8,128)S(1)}, f32[8,128]{1,0:T(8,128)S(1)}, u32[]{:S(2)}, u32[]{:S(2)}) collective-permute-start(f32[8,128]{1,0:T(8,128)S(1)} %add_add_fusion.1), channel_id=1, source_target_pairs={{0,96},{4,228},{8,104},{12,236},{16,112},{20,244},{24,120},{28,252... | collective-permute-start | bytes 12296 | tf_op jit(solution)/shard_map/ppermute | solution.py:126
  83.5 85.6 %collective-permute-start.7 = (f32[8,128]{1,0:T(8,128)S(1)}, f32[8,128]{1,0:T(8,128)S(1)}, u32[]{:S(2)}, u32[]{:S(2)}) collective-permute-start(f32[8,128]{1,0:T(8,128)S(1)} %add_add_fusion.1), channel_id=1, source_target_pairs={{4,132},{12,140},{20,148},{28,156},{36,164},{44,172},{52,180},{60,... | collective-permute-start | bytes 12296 | tf_op jit(solution)/shard_map/ppermute | solution.py:126
  88.9 80.2 %collective-permute-start.8 = (f32[8,128]{1,0:T(8,128)S(1)}, f32[8,128]{1,0:T(8,128)S(1)}, u32[]{:S(2)}, u32[]{:S(2)}) collective-permute-start(f32[8,128]{1,0:T(8,128)S(1)} %add_add_fusion.1), channel_id=1, source_target_pairs={{0,32},{4,164},{8,40},{12,172},{16,48},{20,180},{24,56},{28,188},{... | collective-permute-start | bytes 12296 | tf_op jit(solution)/shard_map/ppermute | solution.py:126
  89.2 79.9 %collective-permute-start.9 = (f32[8,128]{1,0:T(8,128)S(1)}, f32[8,128]{1,0:T(8,128)S(1)}, u32[]{:S(2)}, u32[]{:S(2)}) collective-permute-start(f32[8,128]{1,0:T(8,128)S(1)} %add_add_fusion.1), channel_id=1, source_target_pairs={{0,64},{4,196},{8,72},{12,204},{16,80},{20,212},{24,88},{28,220},{... | collective-permute-start | bytes 12296 | tf_op jit(solution)/shard_map/ppermute | solution.py:126
  169.1 1.7 collective-permute-start.11

commit v5 on v4

v5 whole, which is shorter than its diff:
```python
import functools
import math

import jax
import jax.numpy as jnp
from jax import lax
from jax.experimental import pallas as pl
from jax.experimental.pallas import tpu as pltpu
from jax.sharding import PartitionSpec as P

LANES = 128
INNER = 8
ROUNDS = (4, 4)


def grad_kernel(live_ref, block_ref, rows_ref, weight_ref, out_ref):
    rows = rows_ref[...].astype(jnp.float32)
    row_ids = lax.broadcasted_iota(jnp.int32, rows.shape, 0)
    masked = jnp.where(row_ids < live_ref[0], rows, jnp.zeros_like(rows)).astype(jnp.bfloat16)
    grads = lax.dot_general(
        block_ref[...], masked, (((0,), (0,)), ((), ())), preferred_element_type=jnp.float32
    )
    out_ref[:, 0] = grads.reshape(weight_ref.shape)
    out_ref[:, 1] = weight_ref[...]


def grad_and_weight(block, grad_rows, live, weight):
    rows, width = block.shape
    pieces, piece_rows, hidden = weight.shape
    steps = 2
    tile, group = width // steps, pieces // steps
    return pl.pallas_call(
        grad_kernel,
        grid=(steps,),
        out_shape=jax.ShapeDtypeStruct((pieces, 2, piece_rows, hidden), jnp.float32),
        in_specs=[
            pl.BlockSpec(memory_space=pltpu.SMEM),
            pl.BlockSpec((rows, tile), lambda i: (0, i)),
            pl.BlockSpec((rows, hidden), lambda i: (0, 0)),
            pl.BlockSpec((group, piece_rows, hidden), lambda i: (i, 0, 0)),
        ],
        out_specs=pl.BlockSpec((group, 2, piece_rows, hidden), lambda i: (i, 0, 0, 0)),
        compiler_params=pltpu.CompilerParams(vmem_limit_bytes=56 * 2**20),
        cost_estimate=pl.CostEstimate(
            flops=2 * rows * width * hidden,
            bytes_accessed=2 * rows * (width + hidden) + 12 * width * hidden,
            transcendentals=0,
        ),
    )(live, block, grad_rows, weight)


def sumsq_kernel(slots, partner_ref, grad_ref, out_ref):
    def body(slot, acc):
        raw = grad_ref[slot, 0] + grad_ref[partner_ref[slot], 0]
        return acc + raw * raw

    zero = jnp.zeros(grad_ref.shape[2:], jnp.float32)
    acc = lax.fori_loop(0, slots, body, zero, unroll=4)
    rows, cols = acc.shape
    part = sum(
        acc[r : r + 8, c : c + LANES] for r in range(0, rows, 8) for c in range(0, cols, LANES)
    )
    out_ref[...] = jnp.broadcast_to(0.5 * jnp.sum(part), out_ref.shape)


def choose_kernel(room, chip_ref, core_ref, *refs):
    part_refs, out_ref = refs[:-1], refs[-1]
    for place in range(room):
        core = core_ref[place]
        for k, part_ref in enumerate(part_refs):

            @pl.when(chip_ref[place] == k)
            def _(place=place, core=core, part_ref=part_ref):
                for level in range(out_ref.shape[0]):
                    out_ref[level, place] = part_ref[core, :, level]


def advance(total, weight, first, second):
    first = 0.9 * first + 0.1 * total
    second = 0.95 * second + 0.05 * total * total
    root = jnp.sqrt(second * (1.0 / (1.0 - 0.95**10))) + 1e-08
    step = (first * (1.0 / (1.0 - 0.9**10))) / root
    return weight - 0.1 * (step + 0.3 * weight), first, second


def update_kernel(slots, limit, *refs):
    source_ref, partner_ref, list_ref, count_ref, rank_ref, sum_ref, grad_ref = refs[:7]
    state_refs, out_ref = refs[7:-1], refs[-1]
    clip = jnp.minimum(jnp.float32(1.0), limit / jnp.sqrt(sum_ref[0:1, 0:1] + 1e-06))
    clip = jnp.broadcast_to(clip, (8, grad_ref.shape[3]))

    def gradient(slot, carry):
        source = source_ref[slot]
        other = partner_ref[source]
        for top in range(0, grad_ref.shape[2], 8):
            rows = pl.ds(top, 8)
            out_ref[slot, 0, rows] = clip * (
                grad_ref[source, 0, rows] + grad_ref[other, 0, rows]
            )
        return carry

    lax.fori_loop(0, slots, gradient, 0, unroll=4)

    def update(place, carry):
        slot = list_ref[place]
        source = source_ref[slot]
        rank = rank_ref[source]
        level = source // INNER
        start = 0
        for room, state_ref in zip(ROUNDS, state_refs):

            @pl.when((rank >= start) & (rank < start + room))
            def _(start=start, room=room, state_ref=state_ref):
                spot = jnp.clip(rank - start, 0, room - 1)
                for top in range(0, grad_ref.shape[2], 8):
                    rows = pl.ds(top, 8)
                    state = [grad_ref[source, 1, rows]]
                    state += [state_ref[level, spot, k, rows] for k in range(2)]
                    for k, value in enumerate(advance(out_ref[slot, 0, rows], *state)):
                        out_ref[slot, k, rows] = value

            start += room
        return carry

    lax.fori_loop(0, count_ref[0], update, 0)


def update(states, slots, limit, scalars, sumsq, spread):
    smem = pl.BlockSpec(memory_space=pltpu.SMEM)
    vmem = pl.BlockSpec(memory_space=pltpu.VMEM)
    return pl.pallas_call(
        functools.partial(update_kernel, slots, limit),
        out_shape=jax.ShapeDtypeStruct((slots, 3, *spread.shape[2:]), jnp.float32),
        in_specs=[smem] * len(scalars) + [vmem] * (2 + len(states)),
        out_specs=vmem,
        compiler_params=pltpu.CompilerParams(vmem_limit_bytes=16 * 2**20),
    )(*scalars, sumsq, spread, *states)


def finish_kernel(
    moved_ref, lane_ref, next_first, next_second, weight_ref, first_ref, second_ref, *outs
):
    @pl.when(moved_ref[0] != 0)
    def _():
        for lane, out in zip((lane_ref, next_first, next_second), outs):
            out[...] = lane[:, 0]

    @pl.when(moved_ref[0] == 0)
    def _():
        def one(piece, carry):
            for top in range(0, lane_ref.shape[2], 8):
                rows = pl.ds(top, 8)
                values = advance(
                    lane_ref[piece, 0, rows],
                    weight_ref[piece, rows],
                    first_ref[piece, rows],
                    second_ref[piece, rows],
                )
                for out, value in zip(outs, values):
                    out[piece, rows] = value
            return carry

        lax.fori_loop(0, lane_ref.shape[0], one, 0, unroll=4)


def finish(moved, lanes, blocks):
    slots, _, rows, hidden = lanes.shape
    group = slots // 4

    def lane(k):
        keep = (lambda i, moved: (i, 0, 0, 0)) if k == 0 else None
        index = keep or (lambda i, moved: (i * moved[0], k, 0, 0))
        return pl.BlockSpec((group, 1, rows, hidden), index)

    home = pl.BlockSpec((group, rows, hidden), lambda i, moved: (i * (1 - moved[0]), 0, 0))
    out = pl.BlockSpec((group, rows, hidden), lambda i, moved: (i, 0, 0))
    return pl.pallas_call(
        finish_kernel,
        grid_spec=pltpu.PrefetchScalarGridSpec(
            num_scalar_prefetch=1,
            grid=(slots // group,),
            in_specs=[lane(0), lane(1), lane(2), home, home, home],
            out_specs=[out] * 3,
        ),
        out_shape=[jax.ShapeDtypeStruct((slots, rows, hidden), jnp.float32)] * 3,
        compiler_params=pltpu.CompilerParams(vmem_limit_bytes=56 * 2**20),
    )(moved, lanes, lanes, lanes, *blocks)


def shifted(value, axis, pairs_of):
    total = value
    for pairs in pairs_of:
        total = total + lax.ppermute(value, axis, pairs)
    return total


def plane_sum(value, slots, inner):
    value = shifted(value, "expert", [[(i, i ^ 1) for i in range(slots)]])
    return shifted(
        value,
        "expert",
        [
            [(i, i // inner * inner + (i + k) % inner) for i in range(slots)]
            for k in range(2, inner, 2)
        ],
    )


def all_sum(value):
    slots = lax.axis_size("expert")
    width = lax.axis_size("mp")
    value = shifted(
        value, "mp", [[(i, (i + k) % width) for i in range(width)] for k in range(1, width)]
    )
    value = plane_sum(value, slots, INNER)
    half = slots // INNER // 2
    core = lax.axis_index("expert") % 2
    total = jnp.where(core == 0, value, jnp.zeros_like(value))
    for k in range(half):
        spots = [
            (i, (i + (k + i % 2 * half) * INNER) % slots) for i in range(slots) if k + i % 2
        ]
        total = total + lax.ppermute(value, "expert", spots)
    return shifted(total, "expert", [[(i, i ^ 1) for i in range(slots)]])


def pick(array, index, axis):
    return lax.dynamic_index_in_dim(array, index, axis, keepdims=False)


def within_plane(blocks, slots, rows):
    me = lax.axis_index("expert")
    chips = INNER // 2
    chip, core = me // 2 % chips, me % 2
    shape = (slots // INNER, chips, 2, rows, blocks[0].shape[-1])
    views = [block.reshape(shape) for block in blocks]
    other = jnp.stack([pick(view, 1 - core, 2) for view in views])
    mate = lax.ppermute(other, "expert", [(i, i ^ 1) for i in range(slots)])
    parts = []
    for k in range(chips):
        spot = (chip + k) % chips
        own = jnp.stack([pick(pick(view, spot, 1), core, 1) for view in views])
        part = jnp.stack([own, pick(mate, spot, 2)])
        if k:
            spots = [(i, i // INNER * INNER + (i + 2 * k) % INNER) for i in range(slots)]
            part = lax.ppermute(part, "expert", spots)
        parts.append(part)
    return tuple(parts)


def to_pieces(array):
    return lax.all_to_all(array, "expert", split_axis=0, concat_axis=0, tiled=True)


def along_planes(array, slots):
    groups = [[z * INNER + q for z in range(slots // INNER)] for q in range(INNER)]
    return lax.all_to_all(
        array, "expert", split_axis=0, concat_axis=0, tiled=True, axis_index_groups=groups
    )


def gather_states(room, place_slots, parts):
    me = lax.axis_index("expert")
    chip = (me // 2 - place_slots // 2) % (INNER // 2)
    core = (me + place_slots) % 2
    smem = pl.BlockSpec(memory_space=pltpu.SMEM)
    vmem = pl.BlockSpec(memory_space=pltpu.VMEM)
    _, lanes, levels, rows, hidden = parts[0].shape
    return pl.pallas_call(
        functools.partial(choose_kernel, room),
        out_shape=jax.ShapeDtypeStruct((levels, room, lanes, rows, hidden), jnp.float32),
        in_specs=[smem, smem] + [vmem] * len(parts),
        out_specs=vmem,
        compiler_params=pltpu.CompilerParams(vmem_limit_bytes=16 * 2**20),
    )(chip, core, *parts)


def on_device(
    tokens, cotangent, counts, place_now, partner, place_next, weight, first_moment, second_moment
):
    slots = lax.axis_size("expert")
    units = slots // 2
    width_dev = weight.shape[1]
    hidden = weight.shape[2]
    rows = width_dev // slots
    limit = 4.0 * math.sqrt(units * width_dev * lax.axis_size("mp") * hidden)

    pair = jnp.clip(partner, 0, slots - 1)
    equal = place_now[None, :] == place_next[:, None]
    lowest = jnp.argmax(equal, axis=1).astype(jnp.int32)
    source = jnp.where(place_now == place_next, jnp.arange(slots, dtype=jnp.int32), lowest)

    me = lax.axis_index("expert")
    moved = place_now != place_next
    slot_ids = jnp.arange(slots, dtype=jnp.int32)
    needed = jnp.any((source[None, :] == slot_ids[:, None]) & moved[None, :], axis=1)
    before = (slot_ids[None, :] < slot_ids[:, None]) & (
        slot_ids[None, :] // INNER == slot_ids[:, None] // INNER
    )
    rank = jnp.sum(jnp.where(before & needed[None, :], 1, 0), axis=1).astype(jnp.int32)
    most = jnp.max(jnp.where(needed, rank + 1, 0))
    mine = needed & (slot_ids // INNER == me // INNER)
    order = jnp.arange(INNER, dtype=jnp.int32)
    places = jnp.max(
        jnp.where(mine[None, :] & (rank[None, :] == order[:, None]), slot_ids[None, :], 0), axis=1
    ).astype(jnp.int32)

    moved_rank = jnp.sum(
        jnp.where((slot_ids[None, :] < slot_ids[:, None]) & moved[None, :], 1, 0), axis=1
    )
    moved_list = jnp.max(
        jnp.where(
            moved[None, :] & (moved_rank[None, :] == slot_ids[:, None]), slot_ids[None, :], 0
        ),
        axis=1,
    ).astype(jnp.int32)
    count = jnp.sum(jnp.where(moved, 1, 0)).astype(jnp.int32).reshape(1)

    parts = within_plane((first_moment[0], second_moment[0]), slots, rows)
    blocks = [
        array.reshape(slots, rows, hidden) for array in (weight, first_moment, second_moment)
    ]
    spread = to_pieces(grad_and_weight(tokens[0], cotangent[0], counts, blocks[0]))
    chosen = gather_states(ROUNDS[0], places[: ROUNDS[0]], parts)
    spread, chosen = lax.optimization_barrier((spread, chosen))
    states = along_planes(chosen, slots)

    smem = pl.BlockSpec(memory_space=pltpu.SMEM)
    part = pl.pallas_call(
        functools.partial(sumsq_kernel, slots),
        out_shape=jax.ShapeDtypeStruct((8, LANES), jnp.float32),
        in_specs=[smem, pl.BlockSpec(memory_space=pltpu.VMEM)],
        out_specs=pl.BlockSpec(memory_space=pltpu.VMEM),
        compiler_params=pltpu.CompilerParams(vmem_limit_bytes=8 * 2**20),
        cost_estimate=pl.CostEstimate(
            flops=spread.size, bytes_accessed=spread.size * 4, transcendentals=0
        ),
    )(pair, spread)
    sumsq = all_sum(part)

    scalars = (source, pair, moved_list, count, rank)

    def direct(states, parts, sumsq, spread):
        return update([states], slots, limit, scalars, sumsq, spread)

    def with_rest(states, parts, sumsq, spread):
        rest = along_planes(gather_states(ROUNDS[1], places[ROUNDS[0] :], parts), slots)
        return update([states, rest], slots, limit, scalars, sumsq, spread)

    out = lax.cond(most > ROUNDS[0], with_rest, direct, states, parts, sumsq, spread)
    out = to_pieces(out)
    mine = pick(moved, me, 0).astype(jnp.int32).reshape(1)
    parts = finish(mine, out, blocks)
    return tuple(part.reshape(weight.shape) for part in parts)


def solution(mesh):
    placed = (
        P("expert", None, "mp"),
        P("expert", None, None),
        P("expert"),
        P(),
        P(),
        P(),
        P("expert", "mp", None),
        P("expert", "mp", None),
        P("expert", "mp", None),
    )
    return jax.shard_map(
        on_device,
        mesh=mesh,
        in_specs=placed,
        out_specs=(P("expert", "mp", None), P("expert", "mp", None), P("expert", "mp", None)),
        check_vma=False,
    )
```

time: 292 us -> 267 us (0.914)
  blocking collectives: 115 us -> 0 us
  waiting for transfers between devices: 115 us -> 180 us
  Pallas kernels: 8.62 us -> 18.6 us
  starting transfers between devices: 44.1 us -> 52.9 us
  local copies, waits for them, and re-layouts: 2.3 us -> 6.4 us
    all_to_all x1 -> x0, blocking collectives: 115 us -> none  [to_pieces(): lax.all_to_all(array, 'expert', split_axis=0, concat_axis=0, tiled=True)]
    all_to_all x2, waiting for transfers between devices: 34.4 us -> 104 us  [to_pieces(): lax.all_to_all(array, 'expert', split_axis=0, concat_axis=0, tiled=True)]
    ppermute x4, waiting for transfers between devices: 75.9 us -> 9.15 us  [all_sum(): total = total + lax.ppermute(value, 'expert', spots)]
    ppermute x0 -> x4, waiting for transfers between devices: none -> 60.4 us  [the longest x3 60.4 us: within_plane(): part = lax.ppermute(part, 'expert', spots)]
    pallas_call x2 -> x4, Pallas kernels: 7.69 us -> 17.7 us  [the longest x1 6.07 us: finish(): pl.pallas_call(finish_kernel, grid_spec=pltpu.PrefetchScalarGridSpec(num_...]
    ppermute x0 -> x4, starting transfers between devices: none -> 5.56 us  [the longest x3 5.11 us: within_plane(): part = lax.ppermute(part, 'expert', spots)]
    all_to_all x0 -> x1, starting transfers between devices: none -> 5.51 us  [along_planes(): lax.all_to_all(array, 'expert', split_axis=0, concat_axis=0, tiled=True,...]
    another operation x0 -> x2, local copies, waits for them, and re-layouts: none -> 3.16 us  [the longest x1 1.64 us: within_plane(): own = jnp.stack([pick(pick(view, spot, 1), core, 1) for view in views])]
  transfers between devices with their start and end apart: 14 -> 19, of which waited for: 9 -> 11; matrix products, arithmetic and copies ran while one was open for 2% -> 4% of each run, Pallas kernels for 0% -> 1%
where the time goes in v5:
time: 267 us; the launch traced here: 266 us
  waiting for transfers between devices  180 us (67%)
  starting transfers between devices  52.9 us (20%)
  Pallas kernels  18.6 us (7%)
  local copies, waits for them, and re-layouts  6.4 us (2%)
  other arithmetic  4.41 us (2%)
  between operations  2.83 us (1%)
    all_to_all x2, waiting for transfers between devices, to_pieces(): lax.all_to_all(array, 'expert', split_axis=0, concat_axis=0, tiled=True)  104 us
    ppermute x3, waiting for transfers between devices, within_plane(): part = lax.ppermute(part, 'expert', spots)  60.4 us
    all_to_all x2, starting transfers between devices, to_pieces(): lax.all_to_all(array, 'expert', split_axis=0, concat_axis=0, tiled=True)  19.5 us
    ppermute x4, starting transfers between devices, all_sum(): total = total + lax.ppermute(value, 'expert', spots)  11.4 us
    ppermute x8, starting transfers between devices, shifted(): total = total + lax.ppermute(value, axis, pairs)  10.9 us
    ppermute x4, waiting for transfers between devices, all_sum(): total = total + lax.ppermute(value, 'expert', spots)  9.15 us
    ppermute x8, waiting for transfers between devices, shifted(): total = total + lax.ppermute(value, axis, pairs)  6.89 us
    pallas_call x1, Pallas kernels, finish(): pl.pallas_call(finish_kernel, grid_spec=pltpu.PrefetchScalarGridSpec(num_...  6.07 us
  transfers between devices with their start and end apart: 19, of which 11 were waited for; matrix products, arithmetic and copies ran while one was open for 4% of the time, Pallas kernels for 1%

profile of v5, /device:TPU:1, one launch (start us, length us, event | category | flops | bytes accessed | tf_op | source)
XLA Modules:
  0.0 265.7 jit_solution(6668344431439399468)
XLA Ops:
  1.3 4.3 %shard_map.112 = f32[64,2,24,256]{3,2,1,0:T(8,128)} custom-call(s32[1]{0:T(128)S(6)} %copy.46.live_ref, bf16[1024,1536]{1,0:T(8,128)(2,1)} %bitcast.73, bf16[1024,256]{1,0:T(8,128)(2,1)} %bitcast.76, f32[64,24,256]{2,1,0:T(8,128)} %bitcast.65), custom_call_target="tpu_custom_call" | custom-call | flops 805306368 | bytes 8388608 | tf_op jit(solution)/shard_map/pallas_call | solution.py:32
  5.5 13.0 %all-to-all-start.1 = ((f32[64,2,24,256]{3,2,1,0:T(8,128)}), f32[64,2,24,256]{3,2,1,0:T(8,128)S(1)}, u32[]{:S(2)}, u32[]{:S(2)}) async-start(f32[64,2,24,256]{3,2,1,0:T(8,128)} %shard_map.112), calls=%async_computation.1 | async-start | bytes 6291456 | tf_op jit(solution)/shard_map/all_to_all | solution.py:252
  18.6 1.5 constant_dynamic-slice_fusion
  20.3 1.3 pad_maximum_fusion
  23.7 1.6 dynamic-slice_bitcast_fusion.4
  25.5 1.5 dynamic-slice_bitcast_fusion
  27.1 1.4 collective-permute-start.1
  28.5 2.5 collective-permute-start.2
  31.1 1.3 collective-permute-start.3
  32.6 28.4 %collective-permute-done.1.refs_1_ = f32[2,2,8,24,256]{4,3,2,1,0:T(8,128)S(1)} collective-permute-done((f32[2,2,8,24,256]{4,3,2,1,0:T(8,128)S(1)}, f32[2,2,8,24,256]{4,3,2,1,0:T(8,128)S(1)}, u32[]{:S(2)}, u32[]{:S(2)}) %collective-permute-start.1) | collective-permute-done | bytes 786464 | tf_op jit(solution)/shard_map/ppermute | solution.py:246
  61.0 31.8 %collective-permute-done.2.refs_2_ = f32[2,2,8,24,256]{4,3,2,1,0:T(8,128)S(1)} collective-permute-done((f32[2,2,8,24,256]{4,3,2,1,0:T(8,128)S(1)}, f32[2,2,8,24,256]{4,3,2,1,0:T(8,128)S(1)}, u32[]{:S(2)}, u32[]{:S(2)}) %collective-permute-start.2) | collective-permute-done | bytes 786464 | tf_op jit(solution)/shard_map/ppermute | solution.py:246
  94.0 1.9 shard_map.113
  95.9 5.5 %all-to-all-start.2 = ((f32[8,4,2,24,256]{4,3,2,1,0:T(8,128)}), f32[8,4,2,24,256]{4,3,2,1,0:T(8,128)}, u32[]{:S(2)}, u32[]{:S(2)}) async-start(f32[8,4,2,24,256]{4,3,2,1,0:T(8,128)} %shard_map.113), calls=%async_computation.2 | async-start | bytes 3145728 | tf_op jit(solution)/shard_map/all_to_all | solution.py:257
  101.4 0.9 shard_map.114
  102.4 2.8 %collective-permute-start.6 = (f32[8,128]{1,0:T(8,128)S(1)}, f32[8,128]{1,0:T(8,128)S(1)}, u32[]{:S(2)}, u32[]{:S(2)}) collective-permute-start(f32[8,128]{1,0:T(8,128)S(1)} %shard_map.114), channel_id=1, source_target_pairs={{0,3},{1,0},{2,1},{3,2},{4,7},{5,4},{6,5},{7,6},{8,11},{9,8},{10,9... | collective-permute-start | bytes 12296 | tf_op jit(solution)/shard_map/ppermute | solution.py:193
  106.2 2.9 %collective-permute-done.5 = f32[8,128]{1,0:T(8,128)S(1)} collective-permute-done((f32[8,128]{1,0:T(8,128)S(1)}, f32[8,128]{1,0:T(8,128)S(1)}, u32[]{:S(2)}, u32[]{:S(2)}) %collective-permute-start.5) | collective-permute-done | bytes 4128 | tf_op jit(solution)/shard_map/ppermute | solution.py:193
  109.2 2.7 %collective-permute-start.7 = (f32[8,128]{1,0:T(8,128)S(1)}, f32[8,128]{1,0:T(8,128)S(1)}, u32[]{:S(2)}, u32[]{:S(2)}) collective-permute-start(f32[8,128]{1,0:T(8,128)S(1)} %add_add_fusion.2), channel_id=1, source_target_pairs={{0,4},{4,0},{8,12},{12,8},{16,20},{20,16},{24,28},{28,24},{32,36},... | collective-permute-start | bytes 12296 | tf_op jit(solution)/shard_map/ppermute | solution.py:193
  113.0 1.9 collective-permute-start.9
  115.9 1.5 collective-permute-done.9
  117.4 1.6 collective-permute-done.8
  119.0 2.9 %collective-permute-start.14 = (f32[8,128]{1,0:T(8,128)S(1)}, f32[8,128]{1,0:T(8,128)S(1)}, u32[]{:S(2)}, u32[]{:S(2)}) collective-permute-start(f32[8,128]{1,0:T(8,128)S(1)} %add_add_fusion.1), channel_id=1, source_target_pairs={{0,96},{4,228},{8,104},{12,236},{16,112},{20,244},{24,120},{28,252... | collective-permute-start | bytes 12296 | tf_op jit(solution)/shard_map/ppermute | solution.py:223
  122.0 2.1 collective-permute-start.13
  124.1 1.2 collective-permute-start.12
  125.2 5.2 %collective-permute-start.11 = (f32[8,128]{1,0:T(8,128)S(1)}, f32[8,128]{1,0:T(8,128)S(1)}, u32[]{:S(2)}, u32[]{:S(2)}) collective-permute-start(f32[8,128]{1,0:T(8,128)S(1)} %add_add_fusion.1), channel_id=1, source_target_pairs={{4,132},{12,140},{20,148},{28,156},{36,164},{44,172},{52,180},{60,... | collective-permute-start | bytes 12296 | tf_op jit(solution)/shard_map/ppermute | solution.py:223
  130.6 4.9 %collective-permute-done.14 = f32[8,128]{1,0:T(8,128)S(1)} collective-permute-done((f32[8,128]{1,0:T(8,128)S(1)}, f32[8,128]{1,0:T(8,128)S(1)}, u32[]{:S(2)}, u32[]{:S(2)}) %collective-permute-start.14) | collective-permute-done | bytes 4128 | tf_op jit(solution)/shard_map/ppermute | solution.py:223
  135.5 4.2 %collective-permute-done.11 = f32[8,128]{1,0:T(8,128)S(1)} collective-permute-done((f32[8,128]{1,0:T(8,128)S(1)}, f32[8,128]{1,0:T(8,128)S(1)}, u32[]{:S(2)}, u32[]{:S(2)}) %collective-permute-start.11) | collective-permute-done | bytes 4128 | tf_op jit(solution)/shard_map/ppermute | solution.py:223
  139.7 1.3 collective-permute-start.15
  142.3 5.5 %conditional.1 = (f32[64,3,24,256]{3,2,1,0:T(8,128)}) conditional(s32[]{:T(128)} %convert_element_type.8, (s32[64]{0:T(128)S(1)}, s32[64]{0:T(128)S(1)}, s32[64]{0:T(128)S(1)}, s32[1]{0:T(128)}, s32[64]{0:T(128)S(1)}, /*index=5*/f32[8,128]{1,0:T(8,128)S(1)}, f32[64,2,24,256]{3,2,1,0:T(8,128)S(1)}, f32[8,4,2,24,256]{4,3,2,1,0:T(8,128)}) %tuple.18, ...), branch_computations={%region_8.9_spmd, %region_9.10_spmd} | conditional | flops 174 | bytes 3145974 | solution.py:350
  142.3 5.4 %branch_0_fun.1 = f32[64,3,24,256]{3,2,1,0:T(8,128)} custom-call(s32[64]{0:T(128)S(1)} %get-tuple-element.28.refs_0_, s32[64]{0:T(128)S(1)} %get-tuple-element.46.refs_1_, s32[64]{0:T(128)S(1)} %get-tuple-element.47.refs_2_, s32[1]{0:T(128)} %get-tuple-element.48.refs_3_, s32[64]{0:T(128)S(1)} %get-tuple-element.49.refs_4_, ...), custom_call_target="tpu_custom_call" | custom-call | tf_op jit(solution)/shard_map/cond/branch_0_fun/pallas_call | solution.py:131
  147.8 6.5 %all-to-all-start.3 = ((f32[64,3,24,256]{3,2,1,0:T(8,128)}), f32[64,3,24,256]{3,2,1,0:T(8,128)}, u32[]{:S(2)}, u32[]{:S(2)}) async-start(f32[64,3,24,256]{3,2,1,0:T(8,128)} %get-tuple-element.107), calls=%async_computation.3 | async-start | bytes 9437184 | tf_op jit(solution)/shard_map/all_to_all | solution.py:252
  155.6 104.0 %all-to-all-done.3.lane_ref.next_first.next_second = f32[64,3,24,256]{3,2,1,0:T(8,128)} async-done(((f32[64,3,24,256]{3,2,1,0:T(8,128)}), f32[64,3,24,256]{3,2,1,0:T(8,128)}, u32[]{:S(2)}, u32[]{:S(2)}) %all-to-all-start.3) | async-done | bytes 4718624 | tf_op jit(solution)/shard_map/all_to_all | solution.py:252
  259.6 6.1 %shard_map.115 = (f32[64,24,256]{2,1,0:T(8,128)}, f32[64,24,256]{2,1,0:T(8,128)}, f32[64,24,256]{2,1,0:T(8,128)}) custom-call(s32[1]{0:T(128)S(6)} %convert_element_type.7.moved_ref, f32[64,3,24,256]{3,2,1,0:T(8,128)} %all-to-all-done.3.lane_ref.next_first.next_second, f32[64,3,24,256]{3,2,1,0:T(8,128)} %all-to-all-done.3.lane_ref.next_first.next_second, ...), custom_call_target="tpu_custom_call" | custom-call | tf_op jit(solution)/shard_map/pallas_call | solution.py:177
  (57 shorter events, 8.6 us)
Async XLA Ops:
  5.5 90.3 %all-to-all-start.1 = ((f32[64,2,24,256]{3,2,1,0:T(8,128)}), f32[64,2,24,256]{3,2,1,0:T(8,128)S(1)}, u32[]{:S(2)}, u32[]{:S(2)}) async-start(f32[64,2,24,256]{3,2,1,0:T(8,128)} %shard_map.112), calls=%async_computation.1 | async-start | bytes 6291456 | tf_op jit(solution)/shard_map/all_to_all | solution.py:252
  20.2 1.8 copy-start.4
  20.3 1.8 copy-start.5
  21.6 3.9 %collective-permute-start = (f32[2,8,4,24,256]{4,3,1,0,2:T(8,128)}, f32[2,8,4,24,256]{4,3,1,0,2:T(8,128)}, u32[]{:S(2)}, u32[]{:S(2)}) collective-permute-start(f32[2,8,4,24,256]{4,3,1,0,2:T(8,128)} %pad_maximum_fusion), channel_id=1, source_target_pairs={{0,4},{4,0},{8,12},{12,8},{16,20},{20,16},{24,28},{28,24},{32,36},... | collective-permute-start | bytes 4718600 | tf_op jit(solution)/shard_map/ppermute | solution.py:238
  27.1 33.9 %collective-permute-start.1 = (f32[2,2,8,24,256]{4,3,2,1,0:T(8,128)S(1)}, f32[2,2,8,24,256]{4,3,2,1,0:T(8,128)S(1)}, u32[]{:S(2)}, u32[]{:S(2)}) collective-permute-start(f32[2,2,8,24,256]{4,3,2,1,0:T(8,128)S(1)} %pad_maximum_fusion.2), channel_id=1, source_target_pairs={{0,8},{4,12},{8,16},{12,20},{16,24},{20,28},{24,0},{28,4},{32,40},... | collective-permute-start | bytes 2359304 | tf_op jit(solution)/shard_map/ppermute | solution.py:246
  28.5 64.3 %collective-permute-start.2 = (f32[2,2,8,24,256]{4,3,2,1,0:T(8,128)S(1)}, f32[2,2,8,24,256]{4,3,2,1,0:T(8,128)S(1)}, u32[]{:S(2)}, u32[]{:S(2)}) collective-permute-start(f32[2,2,8,24,256]{4,3,2,1,0:T(8,128)S(1)} %pad_maximum_fusion.3), channel_id=1, source_target_pairs={{0,16},{4,20},{8,24},{12,28},{16,0},{20,4},{24,8},{28,12},{32,48},... | collective-permute-start | bytes 2359304 | tf_op jit(solution)/shard_map/ppermute | solution.py:246
  31.1 61.9 %collective-permute-start.3 = (f32[2,2,8,24,256]{4,3,2,1,0:T(8,128)S(1)}, f32[2,2,8,24,256]{4,3,2,1,0:T(8,128)S(1)}, u32[]{:S(2)}, u32[]{:S(2)}) collective-permute-start(f32[2,2,8,24,256]{4,3,2,1,0:T(8,128)S(1)} %pad_maximum_fusion.4), channel_id=1, source_target_pairs={{0,24},{4,28},{8,0},{12,4},{16,8},{20,12},{24,16},{28,20},{32,56},... | collective-permute-start | bytes 2359304 | tf_op jit(solution)/shard_map/ppermute | solution.py:246
  32.6 60.4 %copy-start = (f32[2,2,8,24,256]{4,3,2,1,0:T(8,128)}, f32[2,2,8,24,256]{4,3,2,1,0:T(8,128)S(1)}, u32[]{:S(2)}) copy-start(f32[2,2,8,24,256]{4,3,2,1,0:T(8,128)S(1)} %pad_maximum_fusion.1.refs_0_) | copy-start | bytes 2359300
  61.0 32.0 %copy-start.1 = (f32[2,2,8,24,256]{4,3,2,1,0:T(8,128)}, f32[2,2,8,24,256]{4,3,2,1,0:T(8,128)S(1)}, u32[]{:S(2)}) copy-start(f32[2,2,8,24,256]{4,3,2,1,0:T(8,128)S(1)} %collective-permute-done.1.refs_1_) | copy-start | bytes 2359300
  92.8 0.9 copy-start.2
  93.0 1.0 copy-start.3
  95.9 5.5 %copy-start.6 = (s32[64]{0:T(128)S(1)}, s32[64]{0:T(128)}, u32[]{:S(2)}) copy-start(s32[64]{0:T(128)} %param.15) | copy-start | bytes 772
  95.9 46.4 %all-to-all-start.2 = ((f32[8,4,2,24,256]{4,3,2,1,0:T(8,128)}), f32[8,4,2,24,256]{4,3,2,1,0:T(8,128)}, u32[]{:S(2)}, u32[]{:S(2)}) async-start(f32[8,4,2,24,256]{4,3,2,1,0:T(8,128)} %shard_map.113), calls=%async_computation.2 | async-start | bytes 3145728 | tf_op jit(solution)/shard_map/all_to_all | solution.py:257
  102.4 3.9 %collective-permute-start.6 = (f32[8,128]{1,0:T(8,128)S(1)}, f32[8,128]{1,0:T(8,128)S(1)}, u32[]{:S(2)}, u32[]{:S(2)}) collective-permute-start(f32[8,128]{1,0:T(8,128)S(1)} %shard_map.114), channel_id=1, source_target_pairs={{0,3},{1,0},{2,1},{3,2},{4,7},{5,4},{6,5},{7,6},{8,11},{9,8},{10,9... | collective-permute-start | bytes 12296 | tf_op jit(solution)/shard_map/ppermute | solution.py:193
  105.2 4.0 %collective-permute-start.5 = (f32[8,128]{1,0:T(8,128)S(1)}, f32[8,128]{1,0:T(8,128)S(1)}, u32[]{:S(2)}, u32[]{:S(2)}) collective-permute-start(f32[8,128]{1,0:T(8,128)S(1)} %shard_map.114), channel_id=1, source_target_pairs={{0,2},{1,3},{2,0},{3,1},{4,6},{5,7},{6,4},{7,5},{8,10},{9,11},{10,... | collective-permute-start | bytes 12296 | tf_op jit(solution)/shard_map/ppermute | solution.py:193
  105.5 3.7 %collective-permute-start.4 = (f32[8,128]{1,0:T(8,128)S(1)}, f32[8,128]{1,0:T(8,128)S(1)}, u32[]{:S(2)}, u32[]{:S(2)}) collective-permute-start(f32[8,128]{1,0:T(8,128)S(1)} %shard_map.114), channel_id=1, source_target_pairs={{0,1},{1,2},{2,3},{3,0},{4,5},{5,6},{6,7},{7,4},{8,9},{9,10},{10,1... | collective-permute-start | bytes 12296 | tf_op jit(solution)/shard_map/ppermute | solution.py:193
  109.2 3.5 %collective-permute-start.7 = (f32[8,128]{1,0:T(8,128)S(1)}, f32[8,128]{1,0:T(8,128)S(1)}, u32[]{:S(2)}, u32[]{:S(2)}) collective-permute-start(f32[8,128]{1,0:T(8,128)S(1)} %add_add_fusion.2), channel_id=1, source_target_pairs={{0,4},{4,0},{8,12},{12,8},{16,20},{20,16},{24,28},{28,24},{32,36},... | collective-permute-start | bytes 12296 | tf_op jit(solution)/shard_map/ppermute | solution.py:193
  112.7 3.2 %collective-permute-start.10 = (f32[8,128]{1,0:T(8,128)S(1)}, f32[8,128]{1,0:T(8,128)S(1)}, u32[]{:S(2)}, u32[]{:S(2)}) collective-permute-start(f32[8,128]{1,0:T(8,128)S(1)} %add.227), channel_id=1, source_target_pairs={{0,24},{4,28},{8,0},{12,4},{16,8},{20,12},{24,16},{28,20},{32,56},... | collective-permute-start | bytes 12296 | tf_op jit(solution)/shard_map/ppermute | solution.py:193
  113.0 4.4 %collective-permute-start.9 = (f32[8,128]{1,0:T(8,128)S(1)}, f32[8,128]{1,0:T(8,128)S(1)}, u32[]{:S(2)}, u32[]{:S(2)}) collective-permute-start(f32[8,128]{1,0:T(8,128)S(1)} %add.227), channel_id=1, source_target_pairs={{0,16},{4,20},{8,24},{12,28},{16,0},{20,4},{24,8},{28,12},{32,48},... | collective-permute-start | bytes 12296 | tf_op jit(solution)/shard_map/ppermute | solution.py:193
  115.0 4.1 %collective-permute-start.8 = (f32[8,128]{1,0:T(8,128)S(1)}, f32[8,128]{1,0:T(8,128)S(1)}, u32[]{:S(2)}, u32[]{:S(2)}) collective-permute-start(f32[8,128]{1,0:T(8,128)S(1)} %add.227), channel_id=1, source_target_pairs={{0,8},{4,12},{8,16},{12,20},{16,24},{20,28},{24,0},{28,4},{32,40},... | collective-permute-start | bytes 12296 | tf_op jit(solution)/shard_map/ppermute | solution.py:193
  119.0 16.5 %collective-permute-start.14 = (f32[8,128]{1,0:T(8,128)S(1)}, f32[8,128]{1,0:T(8,128)S(1)}, u32[]{:S(2)}, u32[]{:S(2)}) collective-permute-start(f32[8,128]{1,0:T(8,128)S(1)} %add_add_fusion.1), channel_id=1, source_target_pairs={{0,96},{4,228},{8,104},{12,236},{16,112},{20,244},{24,120},{28,252... | collective-permute-start | bytes 12296 | tf_op jit(solution)/shard_map/ppermute | solution.py:223
  122.0 13.5 %collective-permute-start.13 = (f32[8,128]{1,0:T(8,128)S(1)}, f32[8,128]{1,0:T(8,128)S(1)}, u32[]{:S(2)}, u32[]{:S(2)}) collective-permute-start(f32[8,128]{1,0:T(8,128)S(1)} %add_add_fusion.1), channel_id=1, source_target_pairs={{0,64},{4,196},{8,72},{12,204},{16,80},{20,212},{24,88},{28,220},{... | collective-permute-start | bytes 12296 | tf_op jit(solution)/shard_map/ppermute | solution.py:223
  124.1 11.5 %collective-permute-start.12 = (f32[8,128]{1,0:T(8,128)S(1)}, f32[8,128]{1,0:T(8,128)S(1)}, u32[]{:S(2)}, u32[]{:S(2)}) collective-permute-start(f32[8,128]{1,0:T(8,128)S(1)} %add_add_fusion.1), channel_id=1, source_target_pairs={{0,32},{4,164},{8,40},{12,172},{16,48},{20,180},{24,56},{28,188},{... | collective-permute-start | bytes 12296 | tf_op jit(solution)/shard_map/ppermute | solution.py:223
  125.2 14.5 %collective-permute-start.11 = (f32[8,128]{1,0:T(8,128)S(1)}, f32[8,128]{1,0:T(8,128)S(1)}, u32[]{:S(2)}, u32[]{:S(2)}) collective-permute-start(f32[8,128]{1,0:T(8,128)S(1)} %add_add_fusion.1), channel_id=1, source_target_pairs={{4,132},{12,140},{20,148},{28,156},{36,164},{44,172},{52,180},{60,... | collective-permute-start | bytes 12296 | tf_op jit(solution)/shard_map/ppermute | solution.py:223
  139.7 2.6 collective-permute-start.15
  147.8 111.8 %all-to-all-start.3 = ((f32[64,3,24,256]{3,2,1,0:T(8,128)}), f32[64,3,24,256]{3,2,1,0:T(8,128)}, u32[]{:S(2)}, u32[]{:S(2)}) async-start(f32[64,3,24,256]{3,2,1,0:T(8,128)} %get-tuple-element.107), calls=%async_computation.3 | async-start | bytes 9437184 | tf_op jit(solution)/shard_map/all_to_all | solution.py:252
